TPU v7x, 128 devices: a whole 4x4x4 slice. The times are simulated.
128 devices in a mesh: dp: 8 (over x_lo, y), fsdp: 16 (over x_hi, z, core).
Axes of the slice: x: 4 (x_hi: 2, x_lo: 2; x = x_hi * 2 + x_lo), y: 4, z: 4, core: 2. Of those that a mesh axis runs over, the one named last changes fastest.
Arguments:
- grads: bfloat16 [3, 2, 5120, 13824], P(None, None, 'dp', 'fsdp'), may hold values from -6 to 6
- basis_in: float32 [3, 2, 8, 5120, 128], P(None, None, 'dp', 'fsdp'), may hold values from -0.5 to 0.5
- eig_in: float32 [3, 2, 8, 5120], P(None, None, 'dp', 'fsdp'), may hold values from 0.3 to 3
- basis_out: float32 [3, 2, 8, 13824, 288], P(None, None, 'dp', 'fsdp'), may hold values from -0.375 to 0.375
- eig_out: float32 [3, 2, 8, 13824], P(None, None, 'dp', 'fsdp'), may hold values from 0.3 to 3
- owner: int32 [3, 2], replicated, may hold values from 0 to 7
Outputs:
- preconditioned: bfloat16 [3, 2, 5120, 13824], P(None, None, 'dp', 'fsdp')
All inputs are finite; a program needn't handle non-finite values.
Results may differ from a plain program's by a relative error of at most 0.001.
Values sent between devices are 32-bit elements; how exact they have to be, the bound alone decides.
No kernel may reach another device: no remote copies, remote signals or barrier semaphores. Data moves between devices by JAX's collectives and lax.ppermute only.
A program may use at most 128 MiB of HBM per device.

v0:
```python
import jax
import jax.numpy as jnp
from jax import lax
from jax.sharding import PartitionSpec as P

BI = 128
BO = 288


damping = 0.1


def from_root(block, axis, holder):
    block = jnp.where(lax.axis_index(axis) == holder, block, jnp.zeros_like(block))
    return lax.psum(block, axis)


def precondition(gradient, in_basis, in_values, out_basis, out_values):
    in_blocks = gradient.shape[0] // BI
    out_blocks = gradient.shape[1] // BO
    blocked = gradient.astype(jnp.float32).reshape(in_blocks, BI, out_blocks, BO)
    left_basis = in_basis.reshape(in_blocks, BI, BI)
    right_basis = out_basis.reshape(out_blocks, BO, BO)
    left_values = in_values.reshape(in_blocks, BI)
    right_values = out_values.reshape(out_blocks, BO)
    high = lax.Precision.HIGHEST
    turned = jnp.einsum("iak,iaob->ikob", left_basis, blocked, precision=high)
    rotated = jnp.einsum("ikob,obl->ikol", turned, right_basis, precision=high)
    scaled = rotated / (left_values[:, :, None, None] * right_values[None, None, :, :] + damping)
    back_turn = jnp.einsum("ikol,obl->ikob", scaled, right_basis, precision=high)
    result = jnp.einsum("iak,ikob->iaob", left_basis, back_turn, precision=high)
    return result.reshape(gradient.shape).astype(jnp.bfloat16)


def shards(grads, basis_in, eig_in, basis_out, eig_out, owner):
    layer_count = grads.shape[0]
    row_count = grads.shape[2]
    row_index = lax.axis_index("dp")
    layer_results = []
    for layer_slot in range(layer_count):
        matrices = []
        for weight_slot in range(2):
            root_row = owner[layer_slot, weight_slot]
            own_in_basis = basis_in[layer_slot, weight_slot, 0]
            own_in_values = eig_in[layer_slot, weight_slot, 0]
            own_out_basis = basis_out[layer_slot, weight_slot, 0]
            own_out_values = eig_out[layer_slot, weight_slot, 0]
            in_basis, in_values, out_basis, out_values = (
                from_root(own_in_basis, "dp", root_row),
                from_root(own_in_values, "dp", root_row),
                from_root(own_out_basis, "dp", root_row),
                from_root(own_out_values, "dp", root_row),
            )
            whole_basis, whole_values = (
                lax.all_gather(in_basis, "fsdp", axis=0, tiled=True),
                lax.all_gather(in_values, "fsdp", axis=0, tiled=True),
            )
            first_row = row_index * row_count
            mine_basis = lax.dynamic_slice_in_dim(whole_basis, first_row, row_count, 0)
            mine_values = lax.dynamic_slice_in_dim(whole_values, first_row, row_count, 0)
            matrices.append(
                precondition(
                    grads[layer_slot, weight_slot], mine_basis, mine_values, out_basis, out_values
                )
            )
        layer_results.append(jnp.stack(matrices))
    return jnp.stack(layer_results)


def solution(mesh):
    placed = (
        P(None, None, "dp", "fsdp"),
        P(None, None, "dp", "fsdp", None),
        P(None, None, "dp", "fsdp"),
        P(None, None, "dp", "fsdp", None),
        P(None, None, "dp", "fsdp"),
        P(),
    )
    return jax.shard_map(
        shards, mesh=mesh, in_specs=placed, out_specs=P(None, None, "dp", "fsdp"), check_vma=False
    )
```

profile of v0, /device:TPU:0, one launch (start us, length us, event | category | flops | bytes accessed | tf_op | source)
XLA Modules:
  0.0 730.4 jit_solution(16865447536439466379)
XLA Ops:
  11.9 5.2 fusion.79
  38.3 37.0 %all-reduce.7 = (f32[3,288]{1,0:T(4,128)}, f32[320]{0:T(512)S(1)}, f32[320]{0:T(512)S(1)}, f32[320]{0:T(512)S(1)}, f32[320]{0:T(512)S(1)}, /*index=5*/f32[320]{0...) all-reduce(f32[3,288]{1,0:T(4,128)S(1)} %mul.138, ...), channel_id=1, replica_groups=mesh['dp'=8,'fsdp'=16] {'dp'}, use_global_device_ids=true, to_apply=%region_23.24 | all-reduce | flops 7104 | bytes 56832 | tf_op jit(solution)/shard_map/psum | solution.py:15
  77.5 160.8 %all-reduce.14.cloned.1.call-done = (f32[320,128]{1,0:T(8,128)}, f32[3,288,288]{1,2,0:T(8,128)}, f32[320,128]{1,0:T(8,128)}, f32[3,288,288]{1,2,0:T(8,128)}, f32...) async-done(((f32[320,128]{1,0:T(8,128)}, ...) | async-done | bytes 6955024 | tf_op jit(solution)/shard_map/psum | solution.py:15
  241.4 5.5 fusion.78
  246.8 2.8 reshape.218
  249.6 3.8 reshape.221
  253.4 3.8 reshape.224
  257.2 3.7 reshape.227
  263.1 3.0 reshape.233
  266.0 111.8 %all-reduce.12.cloned.1.call-done = (f32[5120]{0:T(1024)}, f32[5120]{0:T(1024)}, f32[5120]{0:T(1024)}, f32[5120]{0:T(1024)}, f32[5120]{0:T(1024)}, /*index=5*/f32[5120]{0:T(1024)}) async-done(((f32[5120]{0:T(1024)}, f32[5120]{0:T(1024)}, f32[5120]{0:T(1024)}, f32[5120]{0:T(1024)}, f32[5120]{0:T(1024)}, /*index=5*/f32[5120]{0:T(1024)}), (f32[5120]{0:T(1024)}, f32[5120]{0:T(1024)}, f32[5120]{0:T(1024)}, ...) | async-done | bytes 122896
  380.8 48.7 %all-gather.7.cloned.1.call-done = f32[5120,128]{1,0:T(8,128)} async-done(((f32[320,128]{1,0:T(8,128)}), f32[5120,128]{1,0:T(8,128)}) %all-gather.7.cloned.1.call-update) | async-done | bytes 2621456 | tf_op jit(solution)/shard_map/all_gather | solution.py:55
  429.5 50.7 %all-gather.9.cloned.1.call-done = f32[5120,128]{1,0:T(8,128)} async-done(((f32[320,128]{1,0:T(8,128)}), f32[5120,128]{1,0:T(8,128)}) %all-gather.9.cloned.1.call-update) | async-done | bytes 2621456 | tf_op jit(solution)/shard_map/all_gather | solution.py:55
  483.3 4.2 bitcast_divide_fusion.5
  487.4 4.3 fusion.22
  494.3 2.6 convert_element_type.85
  496.9 2.7 fusion.62
  499.7 4.2 bitcast_divide_fusion.4
  503.8 4.3 fusion.20
  513.0 17.8 %all-gather.11.cloned.1.call-done = f32[5120,128]{1,0:T(8,128)} async-done(((f32[320,128]{1,0:T(8,128)}), f32[5120,128]{1,0:T(8,128)}) %all-gather.11.cloned.1.call-update) | async-done | bytes 2621456 | tf_op jit(solution)/shard_map/all_gather | solution.py:55
  530.9 50.7 %all-gather.13.cloned.1.call-done = f32[5120,128]{1,0:T(8,128)} async-done(((f32[320,128]{1,0:T(8,128)}), f32[5120,128]{1,0:T(8,128)}) %all-gather.13.cloned.1.call-update) | async-done | bytes 2621456 | tf_op jit(solution)/shard_map/all_gather | solution.py:55
  585.9 4.2 bitcast_divide_fusion.3
  590.1 4.3 fusion.18
  599.5 2.7 fusion.58
  602.2 4.2 bitcast_divide_fusion.2
  606.4 4.3 fusion.16
  615.6 16.8 %all-gather.15.cloned.1.call-done = f32[5120,128]{1,0:T(8,128)} async-done(((f32[320,128]{1,0:T(8,128)}), f32[5120,128]{1,0:T(8,128)}) %all-gather.15.cloned.1.call-update) | async-done | bytes 2621456 | tf_op jit(solution)/shard_map/all_gather | solution.py:55
  632.4 50.8 %all-gather.17.cloned.1.call-done = f32[5120,128]{1,0:T(8,128)} async-done(((f32[320,128]{1,0:T(8,128)}), f32[5120,128]{1,0:T(8,128)}) %all-gather.17.cloned.1.call-update) | async-done | bytes 2621456 | tf_op jit(solution)/shard_map/all_gather | solution.py:55
  687.6 4.2 bitcast_divide_fusion.1
  691.7 4.3 fusion.14
  703.1 4.2 bitcast_divide_fusion
  707.3 4.3 fusion.12
  720.0 3.3 pad_maximum_fusion
  (154 shorter events, 76.9 us)
Async XLA Ops:
  6.5 231.8 %all-reduce.14.cloned.1.call-start = ((), (), s32[]{:S(2)}) async-start(), calls=%async_computation.7 | async-start | bytes 17891328 | tf_op jit(solution)/shard_map/psum | solution.py:15
  30.9 1.6 copy-start.5
  30.9 2.1 copy-start.15
  35.7 2.5 copy-start.23
  35.7 342.2 %all-reduce.12.cloned.1.call-start = ((), (), s32[]{:S(2)}) async-start(), calls=%async_computation.6 | async-start | bytes 245760
  77.5 352.1 %all-gather.7.cloned.1.call-start = ((), (), s32[]{:S(2)}) async-start(), calls=%async_computation | async-start | bytes 2785280 | tf_op jit(solution)/shard_map/all_gather | solution.py:55
  238.4 241.8 %all-gather.9.cloned.1.call-start = ((), (), s32[]{:S(2)}) async-start(), calls=%async_computation.1 | async-start | bytes 2785280 | tf_op jit(solution)/shard_map/all_gather | solution.py:55
  238.9 291.9 %all-gather.11.cloned.1.call-start = ((), (), s32[]{:S(2)}) async-start(), calls=%async_computation.2 | async-start | bytes 2785280 | tf_op jit(solution)/shard_map/all_gather | solution.py:55
  239.5 342.0 %all-gather.13.cloned.1.call-start = ((), (), s32[]{:S(2)}) async-start(), calls=%async_computation.3 | async-start | bytes 2785280 | tf_op jit(solution)/shard_map/all_gather | solution.py:55
  240.1 392.2 %all-gather.15.cloned.1.call-start = ((), (), s32[]{:S(2)}) async-start(), calls=%async_computation.4 | async-start | bytes 2785280 | tf_op jit(solution)/shard_map/all_gather | solution.py:55
  240.9 442.3 %all-gather.17.cloned.1.call-start = ((), (), s32[]{:S(2)}) async-start(), calls=%async_computation.5 | async-start | bytes 2785280 | tf_op jit(solution)/shard_map/all_gather | solution.py:55
  480.2 3.0 copy-start.14
  480.2 3.0 copy-start.25
  480.2 3.0 copy-start.31
  496.9 2.8 copy-start.13
  496.9 2.8 copy-start.24
  496.9 2.8 copy-start.30
  503.8 4.3 copy-start.7
  513.0 72.9 %copy-start.12 = (f32[3,288,288]{1,2,0:T(8,128)S(1)}, f32[3,288,288]{1,2,0:T(8,128)}, u32[]{:S(2)}) copy-start(f32[3,288,288]{1,2,0:T(8,128)} %get-tuple-element.42) | copy-start | bytes 2985988
  513.0 72.9 %copy-start.29 = (f32[3,288]{1,0:T(4,128)S(1)}, f32[3,288]{1,0:T(4,128)}, u32[]{:S(2)}) copy-start(f32[3,288]{1,0:T(4,128)} %get-tuple-element.32) | copy-start | bytes 10372
  599.5 2.8 copy-start.11
  599.5 2.8 copy-start.28
  606.4 4.3 copy-start.8
  615.6 72.0 %copy-start.10 = (f32[3,288,288]{1,2,0:T(8,128)S(1)}, f32[3,288,288]{1,2,0:T(8,128)}, u32[]{:S(2)}) copy-start(f32[3,288,288]{1,2,0:T(8,128)} %get-tuple-element.38) | copy-start | bytes 2985988
  615.6 72.0 %copy-start.27 = (f32[3,288]{1,0:T(4,128)S(1)}, f32[3,288]{1,0:T(4,128)}, u32[]{:S(2)}) copy-start(f32[3,288]{1,0:T(4,128)} %get-tuple-element.30) | copy-start | bytes 10372
  700.9 2.2 copy-start.9
  700.9 2.2 copy-start.26
  707.2 4.3 copy-start.6
  713.5 2.7 copy-start
  716.3 1.6 copy-start.1
  716.3 1.9 copy-start.2
  718.2 1.6 copy-start.4
  (9 other events, 8.4 us)
Sparse Core Ops, SparseCore 0:
  35.8 202.4 all-reduce.13
  241.3 136.5 all-reduce.11
  380.7 48.8 all-gather.6
  432.2 47.9 all-gather.8
  482.8 47.9 all-gather.10
  533.5 47.9 all-gather.12
  584.3 47.9 all-gather.14
  635.1 47.9 all-gather.16
where the time goes:
time: 738 us; the launch traced here: 730 us
  waiting for transfers between devices  510 us (69%)
  local copies, waits for them, and re-layouts  80.1 us (11%)
  matrix products  76.3 us (10%)
  blocking collectives  37 us (5%)
  between operations  18.8 us (3%)
    all_gather x6, waiting for transfers between devices, shards(): lax.all_gather(in_basis, 'fsdp', axis=0, tiled=True)  235 us
    psum x1, waiting for transfers between devices, from_root(): return lax.psum(block, axis)  161 us
    unnamed x9, waiting for transfers between devices  114 us
    psum x1, blocking collectives, from_root(): return lax.psum(block, axis)  37 us
    dot_general x6, matrix products, precondition(): jnp.einsum('ikol,obl->ikob', scaled, right_basis, precision=high)  25.6 us
    dot_general x6, matrix products, precondition(): rotated = jnp.einsum('ikob,obl->ikol', turned, right_basis, precision=high)  25 us
    reshape x6, local copies, waits for them, and re-layouts, precondition(): gradient.astype(jnp.float32).reshape(in_blocks, BI, out_blocks, BO)  19.2 us
    convert_element_type x12, local copies, waits for them, and re-layouts, precondition(): return result.reshape(gradient.shape).astype(jnp.bfloat16)  17.6 us
  transfers between devices with their start and end apart: 8, of which 8 were waited for; matrix products, arithmetic and copies ran while one was open for 13% of the time, Pallas kernels for 0%

commit v1 on v0

v1 whole, which is shorter than its diff:
```python
import jax
import jax.numpy as jnp
from jax import lax
from jax.experimental import pallas as pl
from jax.experimental.pallas import tpu as pltpu
from jax.sharding import PartitionSpec as P

BI = 128
BO = 288
M = 6
damping = 0.1
F32 = jnp.float32
BF16 = jnp.bfloat16

REM = 288
EIG = 336
ROWS = 344
IN_ROWS = 328
LANES_O = (0, 640, 1280)
LANES_R = (384, 1024)

BITS = (lambda v: v >> 2, lambda v: (v ^ (v >> 1)) & 1, lambda v: (v & 3) >> 1)
SWAPS = (lambda v: v ^ 4, lambda v: v ^ 1, lambda v: (v & 4) | (3 - (v & 3)))


def split(x):
    high = x.astype(BF16)
    return high, (x - high.astype(F32)).astype(BF16)


def pack_kernel(bits_ref, basis_ref, eig_ref, *refs):
    keeps, sends, wide = refs[:3], refs[3:6], refs[6]
    lane = lax.broadcasted_iota(jnp.int32, (48, 128), 1)
    wide[...] = jnp.zeros_like(wide)
    for o in range(3):
        first = bits_ref[o] == 0
        rows = slice(BO * o, BO * (o + 1))
        low, high = basis_ref[0, rows, 0:128], basis_ref[0, rows, 128:256]
        wide[:, 0:32] = basis_ref[0, rows, 256:288]
        rest = []
        for h in range(2):
            total = jnp.zeros((48, 128), F32)
            for g in range(6):
                part = wide[48 * g : 48 * (g + 1), :]
                shift = (16 * g - 16 * h) % 128
                if shift:
                    part = pltpu.roll(part, shift, 1)
                total = jnp.where((lane >= 16 * g) & (lane < 16 * g + 16), part, total)
            rest.append(total)
        eigs = eig_ref[0, o, 0], eig_ref[0, o, 1]
        for ref, a, b in ((keeps[o], 0, 1), (sends[o], 1, 0)):
            main = (low, high)
            ref[0, 0:REM, :] = jnp.where(first, main[a], main[b])
            ref[0, REM:EIG, :] = jnp.where(first, rest[a], rest[b])
            ref[0, EIG:ROWS, :] = jnp.where(first, eigs[a], eigs[b])


def pack(bits, basis, eig_rows):
    half = jax.ShapeDtypeStruct((M, ROWS, 128), F32)
    spec = pl.BlockSpec((1, ROWS, 128), lambda m, bits: (m, 0, 0))
    return pl.pallas_call(
        pack_kernel,
        out_shape=[half] * 6,
        grid_spec=pltpu.PrefetchScalarGridSpec(
            num_scalar_prefetch=1,
            grid=(M,),
            in_specs=[
                pl.BlockSpec((1, 3 * BO, BO), lambda m, bits: (m, 0, 0)),
                pl.BlockSpec((1, 3, 2, 8, 128), lambda m, bits: (m, 0, 0, 0, 0)),
            ],
            out_specs=[spec] * 6,
            scratch_shapes=[pltpu.VMEM((BO, 128), F32)],
        ),
        cost_estimate=pl.CostEstimate(flops=0, bytes_accessed=14_000_000, transcendentals=0),
        name="pack",
    )(bits, basis, eig_rows)


def left_kernel(core_ref, *refs):
    mine, other = refs[:3], refs[3:6]
    first_ref, second_ref, a_ref, whole = refs[6:]
    m = pl.program_id(0)
    core0 = core_ref[0] == 0
    for g in range(3):

        @pl.when(m // 2 == g)
        def _():
            x, y = mine[g][0], other[g][0]
            halves = jnp.where(core0, x, y), jnp.where(core0, y, x)
            for c in range(2):
                whole[320 * c : 320 * (c + 1), :] = halves[c][0:320]
                turned = halves[c][320:328].T
                for k, size in ((0, 128), (1, 128), (2, 64)):
                    a_ref[0, 320 * c + 128 * k : 320 * c + 128 * k + size, :] = jnp.broadcast_to(
                        turned[0:size, k : k + 1], (size, 128)
                    )

    for i in range(5):
        basis = whole[BI * i : BI * (i + 1), :]
        for ref, value in ((first_ref, basis.T), (second_ref, basis)):
            high, low = split(value)
            ref[0, i, 0:128, 0:128] = high
            ref[0, i, 0:128, 128:256] = high
            ref[0, i, 128:256, 0:128] = low
            ref[0, i, 128:256, 128:256] = low


def prepare_left(core, mine, other):
    def pick(g):
        return pl.BlockSpec((1, IN_ROWS, 128), lambda m, core: (jnp.clip(m - 2 * g, 0, 1), 0, 0))

    stacked = jax.ShapeDtypeStruct((M, 5, 256, 256), BF16)
    stacked_spec = pl.BlockSpec((1, 5, 256, 256), lambda m, core: (m, 0, 0, 0))
    return pl.pallas_call(
        left_kernel,
        out_shape=[stacked, stacked, jax.ShapeDtypeStruct((M, 640, 128), F32)],
        grid_spec=pltpu.PrefetchScalarGridSpec(
            num_scalar_prefetch=1,
            grid=(M,),
            in_specs=[pick(g) for g in (0, 1, 2, 0, 1, 2)],
            out_specs=[stacked_spec, stacked_spec, pl.BlockSpec((1, 640, 128), lambda m, core: (m, 0, 0))],
            scratch_shapes=[pltpu.VMEM((640, 128), F32)],
        ),
        cost_estimate=pl.CostEstimate(flops=0, bytes_accessed=12_000_000, transcendentals=0),
        name="left",
    )(core, *mine, *other)


def dot(a, b):
    return jnp.dot(a, b, preferred_element_type=F32)


def dot_nt(a, b):
    return lax.dot_general(a, b, (((1,), (1,)), ((), ())), preferred_element_type=F32)


def half_chain(grad_ref, halves, first_ref, a_ref, mains, rest, right, turned, stacked):
    lane = lax.broadcasted_iota(jnp.int32, (48, 128), 1)
    lane_b = lax.broadcasted_iota(jnp.int32, (BO, 128), 1)

    @pl.when(pl.program_id(0) == 0)
    def _():
        for ref in (*mains, right):
            ref[...] = jnp.zeros_like(ref)

    eig_rest = jnp.zeros((1, 128), F32)
    eigs = []
    for o in range(3):
        rows = slice(BO * o, BO * (o + 1))
        high, low = split(halves[o][0, 0:REM, :])
        mains[o][32 * o : 32 * o + BO, 0:128] = high
        mains[o][32 * o : 32 * o + BO, 128:256] = low
        at = LANES_O[o]
        right[rows, at : at + 128] = high
        right[rows, at + 128 : at + 256] = high
        right[rows, at + 256 : at + 384] = low
        packed = halves[o][0, REM:EIG, :]
        parts = []
        for g in range(6):
            near = (16 * o - 16 * g) % 128
            part = pltpu.roll(packed, near, 1) if near else packed
            far = pltpu.roll(packed, (near + 64) % 128, 1) if (near + 64) % 128 else packed
            part = jnp.where((lane >= 16 * o) & (lane < 16 * o + 16), part, 0.0)
            parts.append(jnp.where((lane >= 64 + 16 * o) & (lane < 80 + 16 * o), far, part))
        rest_high, rest_low = split(jnp.concatenate(parts, axis=0))
        rest[rows, 0:128] = rest_high
        rest[rows, 128:256] = rest_low
        mixed = jnp.where(lane_b < 64, rest_high.astype(F32), rest_low.astype(F32)).astype(BF16)
        for start in LANES_R:
            right[rows, start : start + 128] = mixed
            right[rows, start + 128 : start + 256] = mixed
        eigs.append(halves[o][0, EIG : EIG + 1, :])
        eig_rest = eig_rest + halves[o][0, EIG + 1 : EIG + 2, :]
    eigs.append(eig_rest)

    for o in range(4):
        if o < 3:
            product = dot(grad_ref[0, :, 256 * o : min(256 * o + 384, 864)], mains[o][...])
        else:
            product = dot(grad_ref[0], rest[...])
        high, low = split(product[:, 0:128] + product[:, 128:256])
        for i in range(5):
            turned[i, 0:128, 128 * o : 128 * (o + 1)] = high[BI * i : BI * (i + 1)]
            turned[i, 128:256, 128 * o : 128 * (o + 1)] = low[BI * i : BI * (i + 1)]

    for i in range(5):
        rows = slice(BI * i, BI * (i + 1))
        product = dot(first_ref[0, i], turned[i])
        rotated = product[0:128] + product[128:256]
        a = a_ref[0, rows, :]
        for o in range(4):
            scaled = rotated[:, 128 * o : 128 * (o + 1)] / (a * eigs[o] + damping)
            high, low = split(scaled)
            if o < 3:
                at = LANES_O[o]
                stacked[rows, at : at + 128] = high
                stacked[rows, at + 128 : at + 256] = low
                stacked[rows, at + 256 : at + 384] = high
            else:
                for at in LANES_R:
                    stacked[rows, at : at + 128] = high
                    stacked[rows, at + 128 : at + 256] = low

    for columns, lanes in (
        (slice(0, 256), slice(0, 640)),
        (slice(256, 512), slice(0, 1024)),
        (slice(512, 768), slice(640, 1664)),
        (slice(768, 864), slice(1024, 1664)),
    ):
        yield columns, dot_nt(stacked[:, lanes], right[columns, lanes])


def mine_kernel(grad_ref, h0, h1, h2, first_ref, a_ref, out_ref, m0, m1, m2, rest, right, turned, stacked):
    scratch = (m0, m1, m2), rest, right, turned, stacked
    for columns, value in half_chain(grad_ref, (h0, h1, h2), first_ref, a_ref, *scratch):
        out_ref[0, :, columns] = value


def other_kernel(
    grad_ref, h0, h1, h2, first_ref, a_ref, second_ref, part_ref, out_ref, m0, m1, m2, rest, right, turned, stacked, back
):
    scratch = (m0, m1, m2), rest, right, turned, stacked
    for columns, value in half_chain(grad_ref, (h0, h1, h2), first_ref, a_ref, *scratch):
        high, low = split(value + part_ref[0, :, columns])
        for i in range(5):
            back[i, 0:128, columns] = high[BI * i : BI * (i + 1)]
            back[i, 128:256, columns] = low[BI * i : BI * (i + 1)]
    for i in range(5):
        product = dot(second_ref[0, i], back[i])
        out_ref[0, BI * i : BI * (i + 1), :] = (product[0:128] + product[128:256]).astype(BF16)


def block(*shape):
    return pl.BlockSpec((1, *shape), lambda m: (m,) + (0,) * len(shape))


CHAIN_SCRATCH = [
    pltpu.VMEM((384, 256), BF16),
    pltpu.VMEM((384, 256), BF16),
    pltpu.VMEM((352, 256), BF16),
    pltpu.VMEM((864, 256), BF16),
    pltpu.VMEM((864, 1664), BF16),
    pltpu.VMEM((5, 256, 512), BF16),
    pltpu.VMEM((640, 1664), BF16),
]
CHAIN_IN = [block(640, 864)] + [block(ROWS, 128)] * 3 + [block(5, 256, 256), block(640, 128)]
CHAIN_PARAMS = pltpu.CompilerParams(vmem_limit_bytes=44 * 2**20)


def chain_mine(grads, halves, first, a):
    return pl.pallas_call(
        mine_kernel,
        out_shape=jax.ShapeDtypeStruct((M, 640, 864), F32),
        grid=(M,),
        in_specs=CHAIN_IN,
        out_specs=block(640, 864),
        scratch_shapes=CHAIN_SCRATCH,
        compiler_params=CHAIN_PARAMS,
        cost_estimate=pl.CostEstimate(flops=16_000_000_000, bytes_accessed=30_000_000, transcendentals=0),
        name="mine",
    )(grads, *halves, first, a)


def chain_other(grads, halves, first, a, second, part):
    return pl.pallas_call(
        other_kernel,
        out_shape=jax.ShapeDtypeStruct((M, 640, 864), BF16),
        grid=(M,),
        in_specs=CHAIN_IN + [block(5, 256, 256), block(640, 864)],
        out_specs=block(640, 864),
        scratch_shapes=CHAIN_SCRATCH + [pltpu.VMEM((5, 256, 864), BF16)],
        compiler_params=CHAIN_PARAMS,
        cost_estimate=pl.CostEstimate(flops=20_000_000_000, bytes_accessed=40_000_000, transcendentals=0),
        name="other",
    )(grads, *halves, first, a, second, part)


def eig_out_rows(eig):
    eig = eig.reshape(M, 3, BO)
    main = eig[:, :, :256].reshape(M, 3, 2, 1, 128)
    tail = eig[:, :, 256:].reshape(M, 3, 2, 1, 16)
    rows = []
    for o in range(3):
        once = jnp.pad(tail[:, o], ((0, 0), (0, 0), (0, 0), (16 * o, 48 - 16 * o)))
        rows.append(jnp.concatenate([once, once], axis=-1))
    tail = jnp.stack(rows, axis=1)
    return jnp.concatenate([main, tail, jnp.zeros((M, 3, 2, 6, 128), F32)], axis=3)


def shards(grads, basis_in, eig_in, basis_out, eig_out, owner):
    row = lax.axis_index("dp")
    column = lax.axis_index("fsdp")
    owner = owner.reshape(M)

    def exchange(x, axis, d):
        if axis == "dp":
            pairs = [(v, SWAPS[d](v)) for v in range(8)]
        else:
            pairs = [(f, 2 * SWAPS[d](f >> 1) + (f & 1)) for f in range(16)]
        return lax.ppermute(x, axis, pairs)

    def same_side(d, place, which=slice(None)):
        return (BITS[d](owner[which]) == BITS[d](place))[:, None, None]

    eig_rows = jnp.pad(eig_in.reshape(M, 320), ((0, 0), (0, 704))).reshape(M, 8, 128)
    in_copy = jnp.concatenate([basis_in.reshape(M, 320, 128), eig_rows], axis=1)
    flip = [(d * 16 + q * 2 + c, q * 16 + d * 2 + c) for d in range(8) for q in range(8) for c in range(2)]
    in_copy = lax.ppermute(in_copy, ("dp", "fsdp"), flip)

    bits = jnp.stack([BITS[d](row) for d in range(3)]).astype(jnp.int32)
    packed = pack(bits, basis_out.reshape(M, 3 * BO, BO), eig_out_rows(eig_out))
    keep, send = packed[:3], packed[3:]
    out = [exchange(send[o], "dp", o) for o in range(3)]
    out = [jnp.where(same_side(o, row), keep[o], out[o]) for o in range(3)]
    place = column >> 1
    inner = [in_copy[2 * g : 2 * g + 2] for g in range(3)]
    for step in range(3):
        for g in range(3):
            d = (g + step) % 3
            there = exchange(inner[g], "fsdp", d)
            inner[g] = jnp.where(same_side(d, place, slice(2 * g, 2 * g + 2)), inner[g], there)
        if step < 2:
            for o in range(3):
                d = (o + step + 1) % 3
                there = exchange(out[o], "dp", d)
                out[o] = jnp.where(same_side(d, row), out[o], there)
    across = [lax.ppermute(x, "fsdp", [(f, f ^ 1) for f in range(16)]) for x in inner]
    rest = [exchange(out[o], "dp", o) for o in range(3)]
    first, second, a = prepare_left((column & 1).reshape(1).astype(jnp.int32), inner, across)
    flat = grads.reshape(M, 640, 864)
    part = chain_mine(flat, out, first, a)
    result = chain_other(flat, rest, first, a, second, part)
    return result.reshape(grads.shape)


def solution(mesh):
    placed = (
        P(None, None, "dp", "fsdp"),
        P(None, None, "dp", "fsdp", None),
        P(None, None, "dp", "fsdp"),
        P(None, None, "dp", "fsdp", None),
        P(None, None, "dp", "fsdp"),
        P(),
    )
    return jax.shard_map(
        shards, mesh=mesh, in_specs=placed, out_specs=P(None, None, "dp", "fsdp"), check_vma=False
    )
```

time: 738 us -> 301 us (0.41)
  waiting for transfers between devices: 510 us -> 129 us
  matrix products: 76.3 us -> 0 us
  Pallas kernels: 0 us -> 62.4 us
  starting transfers between devices: 0.74 us -> 60.7 us
  local copies, waits for them, and re-layouts: 80.1 us -> 31.8 us
  blocking collectives: 37 us -> 0 us
  between operations: 18.8 us -> 0.24 us
    all_gather x6 -> x0, waiting for transfers between devices: 235 us -> none  [shards(): lax.all_gather(in_basis, 'fsdp', axis=0, tiled=True)]
    psum x1 -> x0, waiting for transfers between devices: 161 us -> none  [from_root(): return lax.psum(block, axis)]
    ppermute x0 -> x25, waiting for transfers between devices: none -> 129 us  [the longest x21 129 us: exchange(): return lax.ppermute(x, axis, pairs)]
    unnamed x9 -> x0, waiting for transfers between devices: 114 us -> none
    dot_general x24 -> x0, matrix products: 76.3 us -> none  [the longest x6 25.6 us: precondition(): jnp.einsum('ikol,obl->ikob', scaled, right_basis, precision=high)]
    pallas_call x0 -> x4, Pallas kernels: none -> 62.4 us  [the longest x1 25.5 us: chain_other(): pl.pallas_call(other_kernel, out_shape=jax.ShapeDtypeStruct((M, 640, 864)...]
    ppermute x0 -> x25, starting transfers between devices: none -> 60.7 us  [the longest x21 58.3 us: exchange(): return lax.ppermute(x, axis, pairs)]
    psum x1 -> x0, blocking collectives: 37 us -> none  [from_root(): return lax.psum(block, axis)]
  transfers between devices with their start and end apart: 8 -> 25, of which waited for: 8 -> 11; matrix products, arithmetic and copies ran while one was open for 13% -> 7% of each run, Pallas kernels for 0% -> 10%
where the time goes in v1:
time: 301 us; the launch traced here: 297 us
  waiting for transfers between devices  129 us (43%)
  Pallas kernels  62.4 us (21%)
  starting transfers between devices  60.7 us (20%)
  local copies, waits for them, and re-layouts  31.8 us (11%)
  other arithmetic  12.9 us (4%)
    ppermute x21, waiting for transfers between devices, exchange(): return lax.ppermute(x, axis, pairs)  129 us
    ppermute x21, starting transfers between devices, exchange(): return lax.ppermute(x, axis, pairs)  58.3 us
    pallas_call x1, Pallas kernels, chain_other(): pl.pallas_call(other_kernel, out_shape=jax.ShapeDtypeStruct((M, 640, 864)...  25.5 us
    pallas_call x1, Pallas kernels, chain_mine(): pl.pallas_call(mine_kernel, out_shape=jax.ShapeDtypeStruct((M, 640, 864),...  20.9 us
    unnamed x26, local copies, waits for them, and re-layouts  20.4 us
    reshape x1, local copies, waits for them, and re-layouts, shards(): return result.reshape(grads.shape)  9.7 us
    pallas_call x1, Pallas kernels, pack(): pl.pallas_call(pack_kernel, out_shape=[half] * 6, grid_spec=pltpu.Prefetc...  8.49 us
    pallas_call x1, Pallas kernels, prepare_left(): pl.pallas_call(left_kernel, out_shape=[stacked, stacked, jax.ShapeDtypeSt...  7.51 us
  transfers between devices with their start and end apart: 25, of which 11 were waited for; matrix products, arithmetic and copies ran while one was open for 7% of the time, Pallas kernels for 10%

profile of v1, /device:TPU:0, one launch (start us, length us, event | category | flops | bytes accessed | tf_op | source)
XLA Modules:
  0.0 297.3 jit_solution(12752760435814707194)
XLA Ops:
  1.5 8.1 %copy.16 = f32[3,2,1,864,288]{4,3,1,0,2:T(8,128)} copy(f32[3,2,1,864,288]{3,4,2,1,0:T(8,128)} %param.9) | data formatting | bytes 11943936 | tf_op args[3]
  11.1 8.5 %pack.1 = (f32[6,344,128]{2,1,0:T(8,128)}, f32[6,344,128]{2,1,0:T(8,128)}, f32[6,344,128]{2,1,0:T(8,128)}, f32[6,344,128]{2,1,0:T(8,128)}, f32[6,344,128]{2,1,0:T(8,128)}, /*index=5*/f32[6,344,128]{2,1,0:T(8,128)}) custom-call(s32[3]{0:T(128)} %pad_add_fusion.bits_ref, f32[6,864,288]{2,1,0:T(8,128)} %bitcast.28, f32[6,3,2,8,128]{4,3,2,1,0:T(8,128)} %maximum_maximum_fusion.eig_ref), custom_call_target="tpu_custom_call" | custom-call | bytes 14000000 | tf_op jit(solution)/shard_map/pack/pallas_call | solution.py:61
  19.6 3.1 %collective-permute-start.8 = (f32[6,344,128]{2,1,0:T(8,128)}, f32[6,344,128]{2,1,0:T(8,128)}, u32[]{:S(2)}, u32[]{:S(2)}) collective-permute-start(f32[6,344,128]{2,1,0:T(8,128)} %get-tuple-element.19), channel_id=1, source_target_pairs={{0,48},{16,32},{32,16},{48,0},{64,112},{80,96},{96,80},{112,64},{1... | collective-permute-start | bytes 3170312 | tf_op jit(solution)/shard_map/ppermute | solution.py:300
  23.8 1.9 collective-permute-start.12
  25.7 3.1 %collective-permute-start = (f32[6,344,128]{2,1,0:T(8,128)}, f32[6,344,128]{2,1,0:T(8,128)S(1)}, u32[]{:S(2)}, u32[]{:S(2)}) collective-permute-start(f32[6,344,128]{2,1,0:T(8,128)} %get-tuple-element.15), channel_id=1, source_target_pairs={{0,64},{16,80},{32,96},{48,112},{64,0},{80,16},{96,32},{112,48},{1... | collective-permute-start | bytes 3170312 | tf_op jit(solution)/shard_map/ppermute | solution.py:300
  29.0 39.9 %collective-permute-done.8 = f32[6,344,128]{2,1,0:T(8,128)} collective-permute-done((f32[6,344,128]{2,1,0:T(8,128)}, f32[6,344,128]{2,1,0:T(8,128)}, u32[]{:S(2)}, u32[]{:S(2)}) %collective-permute-start.8) | collective-permute-done | bytes 1056800 | tf_op jit(solution)/shard_map/ppermute | solution.py:300
  70.3 22.2 %collective-permute-start.9 = (f32[6,344,128]{2,1,0:T(8,128)S(1)}, f32[6,344,128]{2,1,0:T(8,128)S(1)}, u32[]{:S(2)}, u32[]{:S(2)}) collective-permute-start(f32[6,344,128]{2,1,0:T(8,128)S(1)} %broadcast_select_fusion.6), channel_id=1, source_target_pairs={{0,64},{16,80},{32,96},{48,112},{64,0},{80,16},{96,32},{112,48},{1... | collective-permute-start | bytes 3170312 | tf_op jit(solution)/shard_map/ppermute | solution.py:300
  93.5 3.3 %collective-permute-start.19 = (f32[2,328,128]{2,1,0:T(8,128)}, f32[2,328,128]{2,1,0:T(8,128)S(1)}, u32[]{:S(2)}, u32[]{:S(2)}) collective-permute-start(f32[2,328,128]{2,1,0:T(8,128)} %get-tuple-element.29), channel_id=1, source_target_pairs={{0,6},{1,7},{2,4},{3,5},{4,2},{5,3},{6,0},{7,1},{8,14},{9,15},{10,... | collective-permute-start | bytes 1007624 | tf_op jit(solution)/shard_map/ppermute | solution.py:300
  96.8 18.3 %collective-permute-done.9 = f32[6,344,128]{2,1,0:T(8,128)S(1)} collective-permute-done((f32[6,344,128]{2,1,0:T(8,128)S(1)}, f32[6,344,128]{2,1,0:T(8,128)S(1)}, u32[]{:S(2)}, u32[]{:S(2)}) %collective-permute-start.9) | collective-permute-done | bytes 1056800 | tf_op jit(solution)/shard_map/ppermute | solution.py:300
  115.1 1.6 broadcast_select_fusion
  116.7 2.0 collective-permute-start.1
  119.2 3.3 %collective-permute-start.13 = (f32[2,328,128]{2,1,0:T(8,128)}, f32[2,328,128]{2,1,0:T(8,128)S(1)}, u32[]{:S(2)}, u32[]{:S(2)}) collective-permute-start(f32[2,328,128]{2,1,0:T(8,128)} %get-tuple-element.31), channel_id=1, source_target_pairs={{0,8},{1,9},{2,10},{3,11},{4,12},{5,13},{6,14},{7,15},{8,0},{9,1},... | collective-permute-start | bytes 1007624 | tf_op jit(solution)/shard_map/ppermute | solution.py:300
  122.5 4.4 %collective-permute-done.16 = f32[2,328,128]{2,1,0:T(8,128)S(1)} collective-permute-done((f32[2,328,128]{2,1,0:T(8,128)}, f32[2,328,128]{2,1,0:T(8,128)S(1)}, u32[]{:S(2)}, u32[]{:S(2)}) %collective-permute-start.16) | collective-permute-done | bytes 335904 | tf_op jit(solution)/shard_map/ppermute | solution.py:300
  127.0 1.7 collective-permute-done.13
  128.8 3.1 %collective-permute-start.20 = (f32[2,328,128]{2,1,0:T(8,128)S(1)}, f32[2,328,128]{2,1,0:T(8,128)S(1)}, u32[]{:S(2)}, u32[]{:S(2)}) collective-permute-start(f32[2,328,128]{2,1,0:T(8,128)S(1)} %get-tuple-element.26), channel_id=1, source_target_pairs={{0,8},{1,9},{2,10},{3,11},{4,12},{5,13},{6,14},{7,15},{8,0},{9,1},... | collective-permute-start | bytes 1007624 | tf_op jit(solution)/shard_map/ppermute | solution.py:300
  131.9 11.2 %collective-permute-done.10 = f32[6,344,128]{2,1,0:T(8,128)} collective-permute-done((f32[6,344,128]{2,1,0:T(8,128)S(1)}, f32[6,344,128]{2,1,0:T(8,128)}, u32[]{:S(2)}, u32[]{:S(2)}) %collective-permute-start.10) | collective-permute-done | bytes 1056800 | tf_op jit(solution)/shard_map/ppermute | solution.py:300
  143.1 20.1 %collective-permute-done.1 = f32[6,344,128]{2,1,0:T(8,128)} collective-permute-done((f32[6,344,128]{2,1,0:T(8,128)S(1)}, f32[6,344,128]{2,1,0:T(8,128)}, u32[]{:S(2)}, u32[]{:S(2)}) %collective-permute-start.1) | collective-permute-done | bytes 1056800 | tf_op jit(solution)/shard_map/ppermute | solution.py:300
  163.2 2.4 broadcast_select_fusion.3
  165.7 3.2 %collective-permute-start.2 = (f32[6,344,128]{2,1,0:T(8,128)S(1)}, f32[6,344,128]{2,1,0:T(8,128)S(1)}, u32[]{:S(2)}, u32[]{:S(2)}) collective-permute-start(f32[6,344,128]{2,1,0:T(8,128)S(1)} %get-tuple-element.46), channel_id=1, source_target_pairs={{0,48},{16,32},{32,16},{48,0},{64,112},{80,96},{96,80},{112,64},{1... | collective-permute-start | bytes 3170312 | tf_op jit(solution)/shard_map/ppermute | solution.py:300
  169.3 3.4 %collective-permute-start.17 = (f32[2,328,128]{2,1,0:T(8,128)S(1)}, f32[2,328,128]{2,1,0:T(8,128)S(1)}, u32[]{:S(2)}, u32[]{:S(2)}) collective-permute-start(f32[2,328,128]{2,1,0:T(8,128)S(1)} %get-tuple-element.28), channel_id=1, source_target_pairs={{0,6},{1,7},{2,4},{3,5},{4,2},{5,3},{6,0},{7,1},{8,14},{9,15},{10,... | collective-permute-start | bytes 1007624 | tf_op jit(solution)/shard_map/ppermute | solution.py:300
  172.7 1.5 collective-permute-start.21
  174.2 5.3 %collective-permute-done.14 = f32[2,328,128]{2,1,0:T(8,128)S(1)} collective-permute-done((f32[2,328,128]{2,1,0:T(8,128)S(1)}, f32[2,328,128]{2,1,0:T(8,128)S(1)}, u32[]{:S(2)}, u32[]{:S(2)}) %collective-permute-start.14) | collective-permute-done | bytes 335904 | tf_op jit(solution)/shard_map/ppermute | solution.py:300
  179.7 3.8 %collective-permute-start.15 = (f32[2,328,128]{2,1,0:T(8,128)S(1)}, f32[2,328,128]{2,1,0:T(8,128)S(1)}, u32[]{:S(2)}, u32[]{:S(2)}) collective-permute-start(f32[2,328,128]{2,1,0:T(8,128)S(1)} %broadcast_select_fusion.16), channel_id=1, source_target_pairs={{0,6},{1,7},{2,4},{3,5},{4,2},{5,3},{6,0},{7,1},{8,14},{9,15},{10,... | collective-permute-start | bytes 1007624 | tf_op jit(solution)/shard_map/ppermute | solution.py:300
  183.5 2.8 collective-permute-start.18
  186.3 6.9 %collective-permute-done.5 = f32[6,344,128]{2,1,0:T(8,128)S(1)} collective-permute-done((f32[6,344,128]{2,1,0:T(8,128)S(1)}, f32[6,344,128]{2,1,0:T(8,128)S(1)}, u32[]{:S(2)}, u32[]{:S(2)}) %collective-permute-start.5) | collective-permute-done | bytes 1056800 | tf_op jit(solution)/shard_map/ppermute | solution.py:300
  193.2 19.2 %collective-permute-done.2 = f32[6,344,128]{2,1,0:T(8,128)S(1)} collective-permute-done((f32[6,344,128]{2,1,0:T(8,128)S(1)}, f32[6,344,128]{2,1,0:T(8,128)S(1)}, u32[]{:S(2)}, u32[]{:S(2)}) %collective-permute-start.2) | collective-permute-done | bytes 1056800 | tf_op jit(solution)/shard_map/ppermute | solution.py:300
  216.4 10.0 %copy.14 = bf16[3,2,640,864]{3,2,1,0:T(8,128)(2,1)} copy(bf16[3,2,640,864]{2,3,1,0:T(8,128)(2,1)} %param.6) | data formatting | bytes 13271040 | tf_op args[0]
  226.4 7.5 %left.1 = (bf16[6,5,256,256]{3,2,1,0:T(8,128)(2,1)}, bf16[6,5,256,256]{3,2,1,0:T(8,128)(2,1)}, f32[6,640,128]{2,1,0:T(8,128)}) custom-call(s32[1]{0:T(128)} %bitcast.13.core_ref, f32[2,328,128]{2,1,0:T(8,128)} %broadcast_select_fusion.17.refs_0_, f32[2,328,128]{2,1,0:T(8,128)} %broadcast_select_fusion.14.refs_1_, f32[2,328,128]{2,1,0:T(8,128)} %copy-done.2, ...), custom_call_target="tpu_custom_call" | custom-call | bytes 12000000 | tf_op jit(solution)/shard_map/left/pallas_call | solution.py:114
  236.8 2.1 copy-done
  238.9 20.9 %mine.1.part_ref = f32[6,640,864]{2,1,0:T(8,128)} custom-call(bf16[6,640,864]{2,1,0:T(8,128)(2,1)} %bitcast.29, f32[6,344,128]{2,1,0:T(8,128)S(1)} %get-tuple-element.50.h0, f32[6,344,128]{2,1,0:T(8,128)S(1)} %broadcast_select_fusion.1.h1, f32[6,344,128]{2,1,0:T(8,128)S(1)} %get-tuple-element.44.h2, bf16[6,5,256,256]{3,2,1,0:T(8,128)(2,1)S(1)} %copy-done, ...), custom_call_target="tpu_custom_call" | custom-call | flops 16000000000 | bytes 30000000 | tf_op jit(solution)/shard_map/mine/pallas_call | solution.py:251
  262.1 25.5 %other.1 = bf16[6,640,864]{2,1,0:T(8,128)(2,1)} custom-call(bf16[6,640,864]{2,1,0:T(8,128)(2,1)} %bitcast.30, f32[6,344,128]{2,1,0:T(8,128)S(1)} %collective-permute-done.3.h0, f32[6,344,128]{2,1,0:T(8,128)S(1)} %collective-permute-done.7.h1, f32[6,344,128]{2,1,0:T(8,128)S(1)} %collective-permute-done.11.h2, bf16[6,5,256,256]{3,2,1,0:T(8,128)(2,1)S(1)} %copy-done, ...), custom_call_target="tpu_custom_call" | custom-call | flops 20000000000 | bytes 40000000 | tf_op jit(solution)/shard_map/other/pallas_call | solution.py:265
  287.6 9.7 %copy.20 = bf16[3,2,640,864]{2,3,1,0:T(8,128)(2,1)} copy(bf16[3,2,640,864]{3,2,1,0:T(8,128)(2,1)} %bitcast.31) | data formatting | bytes 13271040 | tf_op jit(solution)/shard_map/reshape | solution.py:333
  (87 shorter events, 17.3 us)
Async XLA Ops:
  11.1 11.6 %copy-start.9 = (f32[3,2,1,320]{3,2,1,0:T(1,128)S(1)}, f32[3,2,1,320]{3,2,1,0:T(1,128)}, u32[]{:S(2)}) copy-start(f32[3,2,1,320]{3,2,1,0:T(1,128)} %param.8) | copy-start | bytes 23044
  11.1 11.7 %copy-start.7 = (f32[3,2,1,320,128]{4,3,2,1,0:T(8,128)S(1)}, f32[3,2,1,320,128]{4,3,2,1,0:T(8,128)}, u32[]{:S(2)}) copy-start(f32[3,2,1,320,128]{4,3,2,1,0:T(8,128)} %param.7) | copy-start | bytes 2949124
  19.6 49.4 %collective-permute-start.8 = (f32[6,344,128]{2,1,0:T(8,128)}, f32[6,344,128]{2,1,0:T(8,128)}, u32[]{:S(2)}, u32[]{:S(2)}) collective-permute-start(f32[6,344,128]{2,1,0:T(8,128)} %get-tuple-element.19), channel_id=1, source_target_pairs={{0,48},{16,32},{32,16},{48,0},{64,112},{80,96},{96,80},{112,64},{1... | collective-permute-start | bytes 3170312 | tf_op jit(solution)/shard_map/ppermute | solution.py:300
  22.8 46.1 %copy-start.6 = (f32[6,344,128]{2,1,0:T(8,128)S(1)}, f32[6,344,128]{2,1,0:T(8,128)}, u32[]{:S(2)}) copy-start(f32[6,344,128]{2,1,0:T(8,128)} %get-tuple-element.18) | copy-start | bytes 3170308
  23.8 68.7 %collective-permute-start.12 = (f32[6,328,128]{2,1,0:T(8,128)}, f32[6,328,128]{2,1,0:T(8,128)S(1)}, u32[]{:S(2)}, u32[]{:S(2)}) collective-permute-start(f32[6,328,128]{2,1,0:T(8,128)} %pad_maximum_fusion), channel_id=1, source_target_pairs={{0,0},{1,1},{2,16},{3,17},{4,32},{5,33},{6,48},{7,49},{8,64},{9,65... | collective-permute-start | bytes 3022856 | tf_op jit(solution)/shard_map/ppermute | solution.py:308
  25.7 71.1 %collective-permute-start = (f32[6,344,128]{2,1,0:T(8,128)}, f32[6,344,128]{2,1,0:T(8,128)S(1)}, u32[]{:S(2)}, u32[]{:S(2)}) collective-permute-start(f32[6,344,128]{2,1,0:T(8,128)} %get-tuple-element.15), channel_id=1, source_target_pairs={{0,64},{16,80},{32,96},{48,112},{64,0},{80,16},{96,32},{112,48},{1... | collective-permute-start | bytes 3170312 | tf_op jit(solution)/shard_map/ppermute | solution.py:300
  70.3 44.7 %copy-start.4 = (f32[6,344,128]{2,1,0:T(8,128)S(1)}, f32[6,344,128]{2,1,0:T(8,128)}, u32[]{:S(2)}) copy-start(f32[6,344,128]{2,1,0:T(8,128)} %get-tuple-element.14) | copy-start | bytes 3170308
  70.3 44.7 %collective-permute-start.9 = (f32[6,344,128]{2,1,0:T(8,128)S(1)}, f32[6,344,128]{2,1,0:T(8,128)S(1)}, u32[]{:S(2)}, u32[]{:S(2)}) collective-permute-start(f32[6,344,128]{2,1,0:T(8,128)S(1)} %broadcast_select_fusion.6), channel_id=1, source_target_pairs={{0,64},{16,80},{32,96},{48,112},{64,0},{80,16},{96,32},{112,48},{1... | collective-permute-start | bytes 3170312 | tf_op jit(solution)/shard_map/ppermute | solution.py:300
  92.5 39.4 %collective-permute-start.4 = (f32[6,344,128]{2,1,0:T(8,128)}, f32[6,344,128]{2,1,0:T(8,128)}, u32[]{:S(2)}, u32[]{:S(2)}) collective-permute-start(f32[6,344,128]{2,1,0:T(8,128)} %get-tuple-element.17), channel_id=1, source_target_pairs={{0,16},{16,0},{32,48},{48,32},{64,80},{80,64},{96,112},{112,96},{1... | collective-permute-start | bytes 3170312 | tf_op jit(solution)/shard_map/ppermute | solution.py:300
  93.5 25.8 %collective-permute-start.19 = (f32[2,328,128]{2,1,0:T(8,128)}, f32[2,328,128]{2,1,0:T(8,128)S(1)}, u32[]{:S(2)}, u32[]{:S(2)}) collective-permute-start(f32[2,328,128]{2,1,0:T(8,128)} %get-tuple-element.29), channel_id=1, source_target_pairs={{0,6},{1,7},{2,4},{3,5},{4,2},{5,3},{6,0},{7,1},{8,14},{9,15},{10,... | collective-permute-start | bytes 1007624 | tf_op jit(solution)/shard_map/ppermute | solution.py:300
  96.8 18.3 %copy-start.5 = (f32[6,344,128]{2,1,0:T(8,128)}, f32[6,344,128]{2,1,0:T(8,128)S(1)}, u32[]{:S(2)}) copy-start(f32[6,344,128]{2,1,0:T(8,128)S(1)} %collective-permute-done) | copy-start | bytes 3170308
  116.6 26.5 %collective-permute-start.10 = (f32[6,344,128]{2,1,0:T(8,128)S(1)}, f32[6,344,128]{2,1,0:T(8,128)}, u32[]{:S(2)}, u32[]{:S(2)}) collective-permute-start(f32[6,344,128]{2,1,0:T(8,128)S(1)} %get-tuple-element.47), channel_id=1, source_target_pairs={{0,16},{16,0},{32,48},{48,32},{64,80},{80,64},{96,112},{112,96},{1... | collective-permute-start | bytes 3170312 | tf_op jit(solution)/shard_map/ppermute | solution.py:300
  116.7 46.5 %collective-permute-start.1 = (f32[6,344,128]{2,1,0:T(8,128)S(1)}, f32[6,344,128]{2,1,0:T(8,128)}, u32[]{:S(2)}, u32[]{:S(2)}) collective-permute-start(f32[6,344,128]{2,1,0:T(8,128)S(1)} %get-tuple-element.48), channel_id=1, source_target_pairs={{0,16},{16,0},{32,48},{48,32},{64,80},{80,64},{96,112},{112,96},{1... | collective-permute-start | bytes 3170312 | tf_op jit(solution)/shard_map/ppermute | solution.py:300
  119.0 8.0 %collective-permute-start.16 = (f32[2,328,128]{2,1,0:T(8,128)}, f32[2,328,128]{2,1,0:T(8,128)S(1)}, u32[]{:S(2)}, u32[]{:S(2)}) collective-permute-start(f32[2,328,128]{2,1,0:T(8,128)} %get-tuple-element.30), channel_id=1, source_target_pairs={{0,2},{1,3},{2,0},{3,1},{4,6},{5,7},{6,4},{7,5},{8,10},{9,11},{10,... | collective-permute-start | bytes 1007624 | tf_op jit(solution)/shard_map/ppermute | solution.py:300
  119.2 9.4 %collective-permute-start.13 = (f32[2,328,128]{2,1,0:T(8,128)}, f32[2,328,128]{2,1,0:T(8,128)S(1)}, u32[]{:S(2)}, u32[]{:S(2)}) collective-permute-start(f32[2,328,128]{2,1,0:T(8,128)} %get-tuple-element.31), channel_id=1, source_target_pairs={{0,8},{1,9},{2,10},{3,11},{4,12},{5,13},{6,14},{7,15},{8,0},{9,1},... | collective-permute-start | bytes 1007624 | tf_op jit(solution)/shard_map/ppermute | solution.py:300
  128.6 34.6 %copy-start.3 = (f32[6,344,128]{2,1,0:T(8,128)S(1)}, f32[6,344,128]{2,1,0:T(8,128)}, u32[]{:S(2)}) copy-start(f32[6,344,128]{2,1,0:T(8,128)} %get-tuple-element.16) | copy-start | bytes 3170308
  128.8 43.8 %collective-permute-start.20 = (f32[2,328,128]{2,1,0:T(8,128)S(1)}, f32[2,328,128]{2,1,0:T(8,128)S(1)}, u32[]{:S(2)}, u32[]{:S(2)}) collective-permute-start(f32[2,328,128]{2,1,0:T(8,128)S(1)} %get-tuple-element.26), channel_id=1, source_target_pairs={{0,8},{1,9},{2,10},{3,11},{4,12},{5,13},{6,14},{7,15},{8,0},{9,1},... | collective-permute-start | bytes 1007624 | tf_op jit(solution)/shard_map/ppermute | solution.py:300
  165.6 27.6 %collective-permute-start.5 = (f32[6,344,128]{2,1,0:T(8,128)S(1)}, f32[6,344,128]{2,1,0:T(8,128)S(1)}, u32[]{:S(2)}, u32[]{:S(2)}) collective-permute-start(f32[6,344,128]{2,1,0:T(8,128)S(1)} %get-tuple-element.45), channel_id=1, source_target_pairs={{0,48},{16,32},{32,16},{48,0},{64,112},{80,96},{96,80},{112,64},{1... | collective-permute-start | bytes 3170312 | tf_op jit(solution)/shard_map/ppermute | solution.py:300
  165.7 46.7 %collective-permute-start.2 = (f32[6,344,128]{2,1,0:T(8,128)S(1)}, f32[6,344,128]{2,1,0:T(8,128)S(1)}, u32[]{:S(2)}, u32[]{:S(2)}) collective-permute-start(f32[6,344,128]{2,1,0:T(8,128)S(1)} %get-tuple-element.46), channel_id=1, source_target_pairs={{0,48},{16,32},{32,16},{48,0},{64,112},{80,96},{96,80},{112,64},{1... | collective-permute-start | bytes 3170312 | tf_op jit(solution)/shard_map/ppermute | solution.py:300
  168.9 10.6 %collective-permute-start.14 = (f32[2,328,128]{2,1,0:T(8,128)S(1)}, f32[2,328,128]{2,1,0:T(8,128)S(1)}, u32[]{:S(2)}, u32[]{:S(2)}) collective-permute-start(f32[2,328,128]{2,1,0:T(8,128)S(1)} %get-tuple-element.27), channel_id=1, source_target_pairs={{0,2},{1,3},{2,0},{3,1},{4,6},{5,7},{6,4},{7,5},{8,10},{9,11},{10,... | collective-permute-start | bytes 1007624 | tf_op jit(solution)/shard_map/ppermute | solution.py:300
  169.3 14.2 %collective-permute-start.17 = (f32[2,328,128]{2,1,0:T(8,128)S(1)}, f32[2,328,128]{2,1,0:T(8,128)S(1)}, u32[]{:S(2)}, u32[]{:S(2)}) collective-permute-start(f32[2,328,128]{2,1,0:T(8,128)S(1)} %get-tuple-element.28), channel_id=1, source_target_pairs={{0,6},{1,7},{2,4},{3,5},{4,2},{5,3},{6,0},{7,1},{8,14},{9,15},{10,... | collective-permute-start | bytes 1007624 | tf_op jit(solution)/shard_map/ppermute | solution.py:300
  172.7 41.3 %collective-permute-start.21 = (f32[2,328,128]{2,1,0:T(8,128)S(1)}, f32[2,328,128]{2,1,0:T(8,128)S(1)}, u32[]{:S(2)}, u32[]{:S(2)}) collective-permute-start(f32[2,328,128]{2,1,0:T(8,128)S(1)} %broadcast_select_fusion.10), channel_id=1, source_target_pairs={{0,2},{1,3},{2,0},{3,1},{4,6},{5,7},{6,4},{7,5},{8,10},{9,11},{10,... | collective-permute-start | bytes 1007624 | tf_op jit(solution)/shard_map/ppermute | solution.py:300
  179.7 34.6 %collective-permute-start.15 = (f32[2,328,128]{2,1,0:T(8,128)S(1)}, f32[2,328,128]{2,1,0:T(8,128)S(1)}, u32[]{:S(2)}, u32[]{:S(2)}) collective-permute-start(f32[2,328,128]{2,1,0:T(8,128)S(1)} %broadcast_select_fusion.16), channel_id=1, source_target_pairs={{0,6},{1,7},{2,4},{3,5},{4,2},{5,3},{6,0},{7,1},{8,14},{9,15},{10,... | collective-permute-start | bytes 1007624 | tf_op jit(solution)/shard_map/ppermute | solution.py:300
  183.5 32.0 %collective-permute-start.18 = (f32[2,328,128]{2,1,0:T(8,128)S(1)}, f32[2,328,128]{2,1,0:T(8,128)S(1)}, u32[]{:S(2)}, u32[]{:S(2)}) collective-permute-start(f32[2,328,128]{2,1,0:T(8,128)S(1)} %broadcast_select_fusion.13), channel_id=1, source_target_pairs={{0,8},{1,9},{2,10},{3,11},{4,12},{5,13},{6,14},{7,15},{8,0},{9,1},... | collective-permute-start | bytes 1007624 | tf_op jit(solution)/shard_map/ppermute | solution.py:300
  212.8 22.4 %collective-permute-start.6 = (f32[6,344,128]{2,1,0:T(8,128)S(1)}, f32[6,344,128]{2,1,0:T(8,128)}, u32[]{:S(2)}, u32[]{:S(2)}) collective-permute-start(f32[6,344,128]{2,1,0:T(8,128)S(1)} %get-tuple-element.49), channel_id=1, source_target_pairs={{0,64},{16,80},{32,96},{48,112},{64,0},{80,16},{96,32},{112,48},{1... | collective-permute-start | bytes 3170312 | tf_op jit(solution)/shard_map/ppermute | solution.py:300
  214.1 12.3 %copy-start.2 = (f32[2,328,128]{2,1,0:T(8,128)}, f32[2,328,128]{2,1,0:T(8,128)S(1)}, u32[]{:S(2)}) copy-start(f32[2,328,128]{2,1,0:T(8,128)S(1)} %broadcast_select_fusion.11.refs_2_) | copy-start | bytes 1007620
  214.1 12.3 %collective-permute-start.24 = (f32[2,328,128]{2,1,0:T(8,128)S(1)}, f32[2,328,128]{2,1,0:T(8,128)}, u32[]{:S(2)}, u32[]{:S(2)}) collective-permute-start(f32[2,328,128]{2,1,0:T(8,128)S(1)} %broadcast_select_fusion.11.refs_2_), channel_id=1, source_target_pairs={{0,1},{1,0},{2,3},{3,2},{4,5},{5,4},{6,7},{7,6},{8,9},{9,8},{10,11... | collective-permute-start | bytes 1007624 | tf_op jit(solution)/shard_map/ppermute | solution.py:327
  215.1 11.3 %collective-permute-start.22 = (f32[2,328,128]{2,1,0:T(8,128)}, f32[2,328,128]{2,1,0:T(8,128)}, u32[]{:S(2)}, u32[]{:S(2)}) collective-permute-start(f32[2,328,128]{2,1,0:T(8,128)} %broadcast_select_fusion.17.refs_0_), channel_id=1, source_target_pairs={{0,1},{1,0},{2,3},{3,2},{4,5},{5,4},{6,7},{7,6},{8,9},{9,8},{10,11... | collective-permute-start | bytes 1007624 | tf_op jit(solution)/shard_map/ppermute | solution.py:327
  216.4 10.0 %collective-permute-start.23 = (f32[2,328,128]{2,1,0:T(8,128)}, f32[2,328,128]{2,1,0:T(8,128)}, u32[]{:S(2)}, u32[]{:S(2)}) collective-permute-start(f32[2,328,128]{2,1,0:T(8,128)} %broadcast_select_fusion.14.refs_1_), channel_id=1, source_target_pairs={{0,1},{1,0},{2,3},{3,2},{4,5},{5,4},{6,7},{7,6},{8,9},{9,8},{10,11... | collective-permute-start | bytes 1007624 | tf_op jit(solution)/shard_map/ppermute | solution.py:327
  233.9 27.0 %collective-permute-start.11 = (f32[6,344,128]{2,1,0:T(8,128)S(1)}, f32[6,344,128]{2,1,0:T(8,128)S(1)}, u32[]{:S(2)}, u32[]{:S(2)}) collective-permute-start(f32[6,344,128]{2,1,0:T(8,128)S(1)} %get-tuple-element.44.h2), channel_id=1, source_target_pairs={{0,48},{16,32},{32,16},{48,0},{64,112},{80,96},{96,80},{112,64},{1... | collective-permute-start | bytes 3170312 | tf_op jit(solution)/shard_map/ppermute | solution.py:300
  234.3 26.7 %collective-permute-start.3 = (f32[6,344,128]{2,1,0:T(8,128)S(1)}, f32[6,344,128]{2,1,0:T(8,128)S(1)}, u32[]{:S(2)}, u32[]{:S(2)}) collective-permute-start(f32[6,344,128]{2,1,0:T(8,128)S(1)} %get-tuple-element.50.h0), channel_id=1, source_target_pairs={{0,64},{16,80},{32,96},{48,112},{64,0},{80,16},{96,32},{112,48},{1... | collective-permute-start | bytes 3170312 | tf_op jit(solution)/shard_map/ppermute | solution.py:300
  236.5 25.5 %collective-permute-start.7 = (f32[6,344,128]{2,1,0:T(8,128)S(1)}, f32[6,344,128]{2,1,0:T(8,128)S(1)}, u32[]{:S(2)}, u32[]{:S(2)}) collective-permute-start(f32[6,344,128]{2,1,0:T(8,128)S(1)} %broadcast_select_fusion.1.h1), channel_id=1, source_target_pairs={{0,16},{16,0},{32,48},{48,32},{64,80},{80,64},{96,112},{112,96},{1... | collective-permute-start | bytes 3170312 | tf_op jit(solution)/shard_map/ppermute | solution.py:300
  (3 other events, 10.7 us)

commit v2 on v0

v2 whole, which is shorter than its diff:
```python
import jax
import jax.numpy as jnp
from jax import lax
from jax.experimental import pallas as pl
from jax.experimental.pallas import tpu as pltpu
from jax.sharding import PartitionSpec as P

BI = 128
BO = 288
M = 6
damping = 0.1
F32 = jnp.float32
BF16 = jnp.bfloat16

PIECE = 48
WIDE = 896
HALF = 3 * PIECE
IN_ROWS = 336

BITS = (lambda v: v >> 2, lambda v: (v ^ (v >> 1)) & 1, lambda v: (v & 3) >> 1)
SWAPS = (lambda v: v ^ 4, lambda v: v ^ 1, lambda v: (v & 4) | (3 - (v & 3)))


def split(x):
    high = x.astype(BF16)
    return high, (x - high.astype(F32)).astype(BF16)


def dot(a, b):
    return jnp.dot(a, b, preferred_element_type=F32)


def dot_tn(a, b):
    return lax.dot_general(a, b, (((0,), (0,)), ((), ())), preferred_element_type=F32)


def block(*shape):
    return pl.BlockSpec((1, *shape), lambda m, *_: (m,) + (0,) * len(shape))


CHAINS = ((0, 0), (1, 0), (2, 0), (0, 1), (1, 1))
LIST = 7
FINAL = 2 * M
CHAIN = FINAL + 3 * 2 * LIST
OWN = 5 * CHAIN
SIDE = OWN + LIST
FITS = SIDE + 3
SMALL = (3, 4, 5)
WHOLE = (M, M, M)


def table_kernel(owner_ref, place_ref, out_ref):
    def clear(i, carry):
        out_ref[i] = 0
        return carry

    lax.fori_loop(0, FITS + 1, clear, 0)
    owners = [owner_ref[m] for m in range(M)]
    corner = [[BITS[d](v) for v in owners] for d in range(3)]
    for c, (turn, axis) in enumerate(CHAINS):
        at = place_ref[axis]
        seen = [jnp.int32(0)] * 4
        steps, ranks = [], []
        for m in range(M):
            away = [corner[(turn + e) % 3][m] ^ BITS[(turn + e) % 3](at) for e in range(3)]
            step = jnp.where(away[2] == 1, 3, jnp.where(away[1] == 1, 2, away[0]))
            rank = seen[0]
            for k in range(1, 4):
                rank = jnp.where(step == k, seen[k], rank)
            for k in range(4):
                seen[k] = seen[k] + (step == k).astype(jnp.int32)
            out_ref[c * CHAIN + m] = step
            out_ref[c * CHAIN + M + m] = rank
            steps.append(step)
            ranks.append(rank)
        for k in range(1, 4):
            spot = jnp.int32(0)
            base = c * CHAIN + FINAL + 2 * LIST * (k - 1)
            for m in range(M):
                inside = steps[m] < k
                slot = jnp.where(inside, spot, LIST - 1)
                out_ref[base + slot] = steps[m]
                out_ref[base + LIST + slot] = ranks[m]
                if c == 0 and k == 1:
                    out_ref[OWN + slot] = m
                spot = spot + inside.astype(jnp.int32)
    for d in range(3):
        out_ref[SIDE + d] = BITS[d](place_ref[0])
    most = [jnp.int32(0)] * 3
    for m in range(M):
        same = [[(corner[d][m] == corner[d][n]).astype(jnp.int32) for n in range(M)] for d in range(3)]
        node = sum(same[0][n] * same[1][n] * same[2][n] for n in range(M))
        most[0] = jnp.maximum(most[0], node)
        for d in range(3):
            e, f = (d + 1) % 3, (d + 2) % 3
            most[1] = jnp.maximum(most[1], sum(same[e][n] * same[f][n] for n in range(M)))
            most[2] = jnp.maximum(most[2], sum(same[d]))
    fits = (most[0] <= SMALL[0]) & (most[1] <= SMALL[1]) & (most[2] <= SMALL[2])
    out_ref[FITS] = fits.astype(jnp.int32)


def make_tables(owner, place):
    smem = pl.BlockSpec(memory_space=pltpu.SMEM)
    return pl.pallas_call(
        table_kernel,
        out_shape=jax.ShapeDtypeStruct((FITS + 1,), jnp.int32),
        in_specs=[smem, smem],
        out_specs=smem,
        name="tables",
    )(owner, place)


def pack_kernel(table_ref, *refs):
    for t in range(3):
        refs[6 + t][0, :, 0:864] = refs[t][0]
        refs[6 + t][0, :, 864:WIDE] = refs[3 + t][0]


def pack(table, basis, eig, slots, other):
    def rows(t, lanes):
        def place(j, table):
            side = table[SIDE + t]
            return table[OWN + j], 2 * t + (1 - side if other else side), 0

        return pl.BlockSpec((1, PIECE, lanes), place)

    return pl.pallas_call(
        pack_kernel,
        out_shape=[jax.ShapeDtypeStruct((slots, PIECE, WIDE), F32)] * 3,
        grid_spec=pltpu.PrefetchScalarGridSpec(
            num_scalar_prefetch=1,
            grid=(slots,),
            in_specs=[rows(t, 864) for t in range(3)] + [rows(t, 32) for t in range(3)],
            out_specs=[block(PIECE, WIDE)] * 3,
        ),
        cost_estimate=pl.CostEstimate(flops=0, bytes_accessed=1_000_000 * slots, transcendentals=0),
        name="pack",
    )(table, basis, basis, basis, eig, eig, eig)


ANY = pl.BlockSpec(memory_space=pl.ANY)
SMEM = pl.BlockSpec(memory_space=pltpu.SMEM)
VMEM = pl.BlockSpec(memory_space=pltpu.VMEM)


def gather_kernel(slots, table_ref, basis_ref, eig_ref, out_ref, sems):
    copies = []
    for j in range(slots):
        m = table_ref[OWN + j]
        copies.append(pltpu.make_async_copy(basis_ref.at[m], out_ref.at[j, pl.ds(0, 320)], sems.at[2 * j]))
        copies.append(pltpu.make_async_copy(eig_ref.at[m], out_ref.at[j, pl.ds(320, 16)], sems.at[2 * j + 1]))
    for copy in copies:
        copy.start()
    for copy in copies:
        copy.wait()


def gather_own(table, basis, eig, slots):
    return pl.pallas_call(
        lambda *refs: gather_kernel(slots, *refs),
        out_shape=jax.ShapeDtypeStruct((slots, IN_ROWS, 128), F32),
        in_specs=[SMEM, ANY, ANY],
        out_specs=VMEM,
        scratch_shapes=[pltpu.SemaphoreType.DMA((2 * slots,))],
        cost_estimate=pl.CostEstimate(flops=0, bytes_accessed=400_000 * slots, transcendentals=0),
        name="gather",
    )(table, basis, eig)


def route_kernel(chains, step, slots, cut, count, table_ref, *refs):
    sources, outs, sems = refs[: count * len(chains)], refs[count * len(chains) : -1], refs[-1]
    for i, c in enumerate(chains):
        for j in range(slots):
            base = c * CHAIN + (j if step > 3 else FINAL + 2 * LIST * (step - 1) + j)
            arrived, slot = table_ref[base], table_ref[base + (M if step > 3 else LIST)]
            for k in range(count):
                source = sources[count * i + k].at[slot]
                if k == 0 and cut:
                    source = source.at[pl.ds(cut * i, cut)]

                @pl.when(arrived == k)
                def _():
                    pltpu.make_async_copy(source, outs[i].at[j], sems.at[i * slots + j]).start()

    for i in range(len(chains)):
        for j in range(slots):
            pltpu.make_async_copy(outs[i].at[j], outs[i].at[j], sems.at[i * slots + j]).wait()


def route(table, chains, step, slots, sources, shape, cut=0):
    count = len(sources[0])
    flat = [x for chain in sources for x in chain]
    return pl.pallas_call(
        lambda *refs: route_kernel(chains, step, slots, cut, count, *refs),
        out_shape=[jax.ShapeDtypeStruct((slots, *shape), F32)] * len(chains),
        in_specs=[SMEM] + [ANY] * len(flat),
        out_specs=[VMEM] * len(chains),
        scratch_shapes=[pltpu.SemaphoreType.DMA((len(chains) * slots,))],
        cost_estimate=pl.CostEstimate(flops=0, bytes_accessed=400_000 * slots, transcendentals=0),
        name="route",
    )(table, *flat)


def left_kernel(core_ref, *refs):
    mine, other = refs[:2], refs[2:4]
    first_ref, second_ref, a_ref, whole = refs[4:]
    core0 = core_ref[0] == 0
    for g, size in ((0, 168), (1, 152)):
        x, y = mine[g][0], other[g][0]
        low, high = jnp.where(core0, x, y), jnp.where(core0, y, x)
        whole[168 * g : 168 * g + size, :] = low[0:size]
        whole[320 + 168 * g : 320 + 168 * g + size, :] = high[0:size]
    a_ref[0, 0:2, :] = low[152:154]
    a_ref[0, 2:3, :] = low[154:155] + high[152:153]
    a_ref[0, 3:5, :] = high[153:155]
    a_ref[0, 5:8, :] = jnp.zeros((3, 128), F32)

    for i in range(5):
        basis = whole[BI * i : BI * (i + 1), :]
        for ref, value in ((first_ref, basis), (second_ref, basis.T)):
            high, low = split(value)
            for k in range(2):
                ref[0, i, 128 * k : 128 * (k + 1), 0:128] = high
                ref[0, i, 128 * k : 128 * (k + 1), 128:256] = low


def prepare_left(core, mine, other):
    stacked = jax.ShapeDtypeStruct((M, 5, 256, 256), BF16)
    return pl.pallas_call(
        left_kernel,
        out_shape=[stacked, stacked, jax.ShapeDtypeStruct((M, 8, 128), F32)],
        grid_spec=pltpu.PrefetchScalarGridSpec(
            num_scalar_prefetch=1,
            grid=(M,),
            in_specs=[block(IN_ROWS // 2, 128)] * 4,
            out_specs=[block(5, 256, 256), block(5, 256, 256), block(8, 128)],
            scratch_shapes=[pltpu.VMEM((640, 128), F32)],
        ),
        cost_estimate=pl.CostEstimate(flops=0, bytes_accessed=12_000_000, transcendentals=0),
        name="left",
    )(core, *mine, *other)


def half_chain(grad_ref, pieces, first_ref, a_ref, basis, turned, back, scaled):
    eigs = []
    for o in range(3):
        window = jnp.concatenate([ref[0, :, 256 * o : 256 * o + 384] for ref in pieces], axis=0)
        if o:
            window = pltpu.roll(window, 384 - 32 * o, 1)
        high, low = split(window[:, 0:BO])
        basis[o, 0:HALF, :] = high
        basis[o, HALF : 2 * HALF, :] = low
        back[o, 0:HALF, :] = high
        back[o, HALF : 2 * HALF, :] = high
        back[o, 2 * HALF : 3 * HALF, :] = low
        eigs.append(jnp.concatenate([ref[0, :, 768:WIDE][:, 96 + o : 97 + o] for ref in pieces], axis=0))

    for o in range(3):
        product = dot(basis[o], grad_ref[0, BO * o : BO * (o + 1), :])
        high, low = split(product[0:HALF] + product[HALF : 2 * HALF])
        for i in range(5):
            turned[i, HALF * o : HALF * (o + 1), 0:128] = high[:, BI * i : BI * (i + 1)]
            turned[i, HALF * o : HALF * (o + 1), 128:256] = low[:, BI * i : BI * (i + 1)]

    for i in range(5):
        product = dot(turned[i], first_ref[0, i])
        rotated = product[:, 0:128] + product[:, 128:256]
        columns = slice(BI * i, BI * (i + 1))
        for o in range(3):
            part = rotated[HALF * o : HALF * (o + 1)] / (eigs[o] * a_ref[0, i : i + 1, :] + damping)
            high, low = split(part)
            scaled[o, 0:HALF, columns] = high
            scaled[o, HALF : 2 * HALF, columns] = low
            scaled[o, 2 * HALF : 3 * HALF, columns] = high

    for o in range(3):
        yield o, dot_tn(back[o], scaled[o])


def mine_kernel(grad_ref, p0, p1, p2, first_ref, a_ref, out_ref, basis, turned, back, scaled):
    for o, value in half_chain(grad_ref, (p0, p1, p2), first_ref, a_ref, basis, turned, back, scaled):
        out_ref[0, BO * o : BO * (o + 1), :] = value


def other_kernel(
    grad_ref, p0, p1, p2, first_ref, a_ref, second_ref, part_ref, out_ref, basis, turned, back, scaled, whole
):
    for o, value in half_chain(grad_ref, (p0, p1, p2), first_ref, a_ref, basis, turned, back, scaled):
        rows = slice(BO * o, BO * (o + 1))
        high, low = split(value + part_ref[0, rows, :])
        for i in range(5):
            whole[i, rows, 0:128] = high[:, BI * i : BI * (i + 1)]
            whole[i, rows, 128:256] = low[:, BI * i : BI * (i + 1)]
    for i in range(5):
        product = dot(whole[i], second_ref[0, i])
        out_ref[0, :, BI * i : BI * (i + 1)] = (product[:, 0:128] + product[:, 128:256]).astype(BF16)


CHAIN_SCRATCH = [
    pltpu.VMEM((3, 2 * HALF, BO), BF16),
    pltpu.VMEM((5, 3 * HALF, 256), BF16),
    pltpu.VMEM((3, 3 * HALF, BO), BF16),
    pltpu.VMEM((3, 3 * HALF, 640), BF16),
]
CHAIN_IN = [block(864, 640)] + [block(PIECE, WIDE)] * 3 + [block(5, 256, 256), block(8, 128)]
CHAIN_PARAMS = pltpu.CompilerParams(vmem_limit_bytes=40 * 2**20)


def chain_mine(grads, pieces, first, a):
    return pl.pallas_call(
        mine_kernel,
        out_shape=jax.ShapeDtypeStruct((M, 864, 640), F32),
        grid=(M,),
        in_specs=CHAIN_IN,
        out_specs=block(864, 640),
        scratch_shapes=CHAIN_SCRATCH,
        compiler_params=CHAIN_PARAMS,
        cost_estimate=pl.CostEstimate(flops=16_000_000_000, bytes_accessed=30_000_000, transcendentals=0),
        name="mine",
    )(grads, *pieces, first, a)


def chain_other(grads, pieces, first, a, second, part):
    return pl.pallas_call(
        other_kernel,
        out_shape=jax.ShapeDtypeStruct((M, 864, 640), BF16),
        grid=(M,),
        in_specs=CHAIN_IN + [block(5, 256, 256), block(864, 640)],
        out_specs=block(864, 640),
        scratch_shapes=CHAIN_SCRATCH + [pltpu.VMEM((5, 864, 256), BF16)],
        compiler_params=CHAIN_PARAMS,
        cost_estimate=pl.CostEstimate(flops=20_000_000_000, bytes_accessed=40_000_000, transcendentals=0),
        name="other",
    )(grads, *pieces, first, a, second, part)


def exchange(x, axis, d):
    if axis == "dp":
        pairs = [(v, SWAPS[d](v)) for v in range(8)]
    else:
        pairs = [(f, 2 * SWAPS[d](f >> 1) + (f & 1)) for f in range(16)]
    return lax.ppermute(x, axis, pairs)


def together(arrays):
    return list(lax.optimization_barrier(tuple(arrays)))


def precondition(sizes, table, core, grads, basis_in, eig_in, basis, eig_out):
    flip = [(d * 16 + q * 2 + c, q * 16 + d * 2 + c) for d in range(8) for q in range(8) for c in range(2)]
    inner = gather_own(table, basis_in, eig_in, sizes[0])
    inner = lax.ppermute(inner, ("dp", "fsdp"), flip)

    out_chains, in_chains = (0, 1, 2), (3, 4)
    shape, cut = (PIECE, WIDE), IN_ROWS // 2
    held = [[x] for x in pack(table, basis, eig_out, sizes[0], False)]
    send = pack(table, basis, eig_out, sizes[0], True)
    in_held = [[inner], [inner]]
    in_send = [inner[:, cut * g : cut * (g + 1)] for g in range(2)]
    for step in range(1, 4):
        there = together([exchange(send[t], "dp", (t + step - 1) % 3) for t in range(3)])
        for t in range(3):
            held[t].append(there[t])
        in_there = together([exchange(in_send[g], "fsdp", (g + step - 1) % 3) for g in range(2)])
        for g in range(2):
            in_held[g].append(in_there[g])
        slots = sizes[step] if step < 3 else M
        send = route(table, out_chains, step + 1, slots, held, shape)
        in_send = route(table, in_chains, step + 1, slots, in_held, (cut, 128), cut)
    across = [lax.ppermute(x, "fsdp", [(f, f ^ 1) for f in range(16)]) for x in in_send]
    rest = [exchange(send[t], "dp", t) for t in range(3)]
    first, second, a = prepare_left(core, in_send, across)
    part = chain_mine(grads, send, first, a)
    return chain_other(grads, rest, first, a, second, part)


def shards(grads, basis_in, eig_in, basis_out, eig_out, owner):
    row = lax.axis_index("dp")
    column = lax.axis_index("fsdp")
    place, core = column >> 1, column & 1
    table = make_tables(owner.reshape(M), jnp.stack([row, place]).astype(jnp.int32))
    eig_rows = eig_in.reshape(M, 320)
    eig_rows = jnp.where(core == 0, jnp.pad(eig_rows, ((0, 0), (0, 64))), jnp.pad(eig_rows, ((0, 0), (64, 0))))
    eig_rows = jnp.pad(eig_rows.reshape(M, 3, 128), ((0, 0), (0, 13), (0, 0)))
    eig_cols = jnp.pad(jnp.swapaxes(eig_out.reshape(M, 3, BO), 1, 2), ((0, 0), (0, 0), (0, 29)))
    arrays = (
        table,
        core.reshape(1).astype(jnp.int32),
        jnp.swapaxes(grads.reshape(M, 640, 864), 1, 2),
        basis_in.reshape(M, 320, 128),
        eig_rows,
        jnp.swapaxes(basis_out.reshape(M, 864, BO), 1, 2),
        eig_cols,
    )
    result = lax.cond(
        table[FITS] == 1,
        lambda *args: precondition(SMALL, *args),
        lambda *args: precondition(WHOLE, *args),
        *arrays,
    )
    return jnp.swapaxes(result, 1, 2).reshape(grads.shape)


def solution(mesh):
    placed = (
        P(None, None, "dp", "fsdp"),
        P(None, None, "dp", "fsdp", None),
        P(None, None, "dp", "fsdp"),
        P(None, None, "dp", "fsdp", None),
        P(None, None, "dp", "fsdp"),
        P(),
    )
    return jax.shard_map(
        shards, mesh=mesh, in_specs=placed, out_specs=P(None, None, "dp", "fsdp"), check_vma=False
    )
```

time: 738 us -> 163 us (0.22)
  waiting for transfers between devices: 510 us -> 25.9 us
  matrix products: 76.3 us -> 0 us
  Pallas kernels: 0 us -> 73.1 us
  local copies, waits for them, and re-layouts: 80.1 us -> 17.2 us
  starting transfers between devices: 0.74 us -> 42.1 us
  blocking collectives: 37 us -> 0 us
  between operations: 18.8 us -> 0.69 us
    all_gather x6 -> x0, waiting for transfers between devices: 235 us -> none  [shards(): lax.all_gather(in_basis, 'fsdp', axis=0, tiled=True)]
    psum x1 -> x0, waiting for transfers between devices: 161 us -> none  [from_root(): return lax.psum(block, axis)]
    unnamed x9 -> x0, waiting for transfers between devices: 114 us -> none
    dot_general x24 -> x0, matrix products: 76.3 us -> none  [the longest x6 25.6 us: precondition(): jnp.einsum('ikol,obl->ikob', scaled, right_basis, precision=high)]
    pallas_call x0 -> x13, Pallas kernels: none -> 73.1 us  [the longest x6 20.6 us: route(): pl.pallas_call(lambda *refs: route_kernel(chains, step, slots, cut, count...]
    ppermute x0 -> x21, starting transfers between devices: none -> 42.1 us  [the longest x18 39.8 us: exchange(): return lax.ppermute(x, axis, pairs)]
    psum x1 -> x0, blocking collectives: 37 us -> none  [from_root(): return lax.psum(block, axis)]
    reshape x12 -> x4, local copies, waits for them, and re-layouts: 28.8 us -> 0.73 us  [the longest x1 0.59 us: shards(): owner.reshape(M)]
  transfers between devices with their start and end apart: 8 -> 21, of which waited for: 8 -> 11; matrix products, arithmetic and copies ran while one was open for 13% -> 1% of each run, Pallas kernels for 0% -> 27%
where the time goes in v2:
time: 163 us; the launch traced here: 162 us
  Pallas kernels  73.1 us (45%)
  starting transfers between devices  42.1 us (26%)
  waiting for transfers between devices  25.9 us (16%)
  local copies, waits for them, and re-layouts  17.2 us (11%)
  other arithmetic  2.28 us (1%)
    ppermute x18, starting transfers between devices, exchange(): return lax.ppermute(x, axis, pairs)  39.8 us
    ppermute x18, waiting for transfers between devices, exchange(): return lax.ppermute(x, axis, pairs)  23.5 us
    pallas_call x6, Pallas kernels, route(): pl.pallas_call(lambda *refs: route_kernel(chains, step, slots, cut, count...  20.6 us
    pallas_call x1, Pallas kernels, chain_other(): pl.pallas_call(other_kernel, out_shape=jax.ShapeDtypeStruct((M, 864, 640)...  18.6 us
    pallas_call x1, Pallas kernels, chain_mine(): pl.pallas_call(mine_kernel, out_shape=jax.ShapeDtypeStruct((M, 864, 640),...  14.6 us
    cond x48, local copies, waits for them, and re-layouts  13.1 us
    pallas_call x2, Pallas kernels, pack(): pl.pallas_call(pack_kernel, out_shape=[jax.ShapeDtypeStruct((slots, PIECE...  6.9 us
    pallas_call x1, Pallas kernels, prepare_left(): pl.pallas_call(left_kernel, out_shape=[stacked, stacked, jax.ShapeDtypeSt...  6.1 us
  transfers between devices with their start and end apart: 21, of which 11 were waited for; matrix products, arithmetic and copies ran while one was open for 1% of the time, Pallas kernels for 27%

profile of v2, /device:TPU:0, one launch (start us, length us, event | category | flops | bytes accessed | tf_op | source)
XLA Modules:
  0.0 161.7 jit_solution(12805683227877641427)
XLA Ops:
  2.0 3.8 %tables.1 = s32[281]{0:T(512)S(1)} custom-call(s32[6]{0:T(128)} %reshape.31.owner_ref, s32[2]{0:T(128)} %pad_add_fusion.place_ref), custom_call_target="tpu_custom_call" | custom-call | tf_op jit(solution)/shard_map/tables/pallas_call | solution.py:104
  8.8 152.9 %conditional.1 = (bf16[6,864,640]{2,1,0:T(8,128)(2,1)}) conditional(s32[]{:T(128)} %bitcast.2, (s32[281]{0:T(512)S(1)}, f32[6,288,864]{2,1,0:T(8,128)}, f32[6,288,32]{1,2,0:T(8,128)S(1)}, f32[6,320,128]{2,1,0:T(8,128)}, f32[6,16,128]{2,1,0:T(8,128)S(1)}, /*index=5*/s32[1]{0:T(128)}, bf16[6,864,640]{2,1,0:T(8,128)(2,1)}) %tuple.34, (s32[281]{0:T(512)S(1)}, ...), branch_computations={%region_0.1_spmd, %region_1.2_spmd} | conditional | flops 35999997952 | bytes 280326560 | solution.py:395
  9.1 2.5 %gather.3 = f32[3,336,128]{2,1,0:T(8,128)} custom-call(s32[281]{0:T(512)S(1)} %get-tuple-element.83.table_ref.refs_0_, f32[6,320,128]{2,1,0:T(8,128)} %get-tuple-element.111.refs_1_, f32[6,16,128]{2,1,0:T(8,128)S(1)} %get-tuple-element.112.refs_2_), custom_call_target="tpu_custom_call" | custom-call | bytes 1200000 | tf_op jit(solution)/shard_map/cond/branch_1_fun/gather/pallas_call | solution.py:159
  11.6 1.7 %collective-permute-start.33 = (f32[3,336,128]{2,1,0:T(8,128)}, f32[3,336,128]{2,1,0:T(8,128)S(1)}, u32[]{:S(2)}, u32[]{:S(2)}) collective-permute-start(f32[3,336,128]{2,1,0:T(8,128)} %gather.3), channel_id=1, source_target_pairs={{0,0},{1,1},{2,16},{3,17},{4,32},{5,33},{6,48},{7,49},{8,64},{9,65... | collective-permute-start | bytes 1548296 | tf_op jit(solution)/shard_map/cond/branch_1_fun/ppermute | solution.py:352
  14.5 3.5 %pack.7 = (f32[3,48,896]{2,1,0:T(8,128)}, f32[3,48,896]{2,1,0:T(8,128)}, f32[3,48,896]{2,1,0:T(8,128)}) custom-call(s32[281]{0:T(512)S(1)} %get-tuple-element.83.table_ref.refs_0_, f32[6,288,864]{2,1,0:T(8,128)} %get-tuple-element.84.refs_0_.refs_1_.refs_2_, f32[6,288,864]{2,1,0:T(8,128)} %get-tuple-element.84.refs_0_.refs_1_.refs_2_, ...), custom_call_target="tpu_custom_call" | custom-call | bytes 3000000 | tf_op jit(solution)/shard_map/cond/branch_1_fun/pack/pallas_call | solution.py:127
  17.9 3.3 %collective-permute-start.21 = (f32[3,48,896]{2,1,0:T(8,128)}, f32[3,48,896]{2,1,0:T(8,128)S(1)}, u32[]{:S(2)}, u32[]{:S(2)}) collective-permute-start(f32[3,48,896]{2,1,0:T(8,128)} %get-tuple-element.87), channel_id=1, source_target_pairs={{0,64},{16,80},{32,96},{48,112},{64,0},{80,16},{96,32},{112,48},{1... | collective-permute-start | bytes 1548296 | tf_op jit(solution)/shard_map/cond/branch_1_fun/ppermute | solution.py:342
  21.2 2.8 %collective-permute-start.22 = (f32[3,48,896]{2,1,0:T(8,128)}, f32[3,48,896]{2,1,0:T(8,128)S(1)}, u32[]{:S(2)}, u32[]{:S(2)}) collective-permute-start(f32[3,48,896]{2,1,0:T(8,128)} %get-tuple-element.88), channel_id=1, source_target_pairs={{0,16},{16,0},{32,48},{48,32},{64,80},{80,64},{96,112},{112,96},{1... | collective-permute-start | bytes 1548296 | tf_op jit(solution)/shard_map/cond/branch_1_fun/ppermute | solution.py:342
  24.1 4.0 %collective-permute-start.23 = (f32[3,48,896]{2,1,0:T(8,128)}, f32[3,48,896]{2,1,0:T(8,128)S(1)}, u32[]{:S(2)}, u32[]{:S(2)}) collective-permute-start(f32[3,48,896]{2,1,0:T(8,128)} %get-tuple-element.89), channel_id=1, source_target_pairs={{0,48},{16,32},{32,16},{48,0},{64,112},{80,96},{96,80},{112,64},{1... | collective-permute-start | bytes 1548296 | tf_op jit(solution)/shard_map/cond/branch_1_fun/ppermute | solution.py:342
  28.9 13.0 %collective-permute-start.35 = (f32[3,168,128]{2,1,0:T(8,128)}, f32[3,168,128]{2,1,0:T(8,128)S(1)}, u32[]{:S(2)}, u32[]{:S(2)}) collective-permute-start(f32[3,168,128]{2,1,0:T(8,128)} %get-tuple-element.144), channel_id=1, source_target_pairs={{0,2},{1,3},{2,0},{3,1},{4,6},{5,7},{6,4},{7,5},{8,10},{9,11},{10,... | collective-permute-start | bytes 774152 | tf_op jit(solution)/shard_map/cond/branch_1_fun/ppermute | solution.py:342
  42.7 3.4 %pack.6 = (f32[3,48,896]{2,1,0:T(8,128)}, f32[3,48,896]{2,1,0:T(8,128)}, f32[3,48,896]{2,1,0:T(8,128)}) custom-call(s32[281]{0:T(512)S(1)} %get-tuple-element.83.table_ref.refs_0_, f32[6,288,864]{2,1,0:T(8,128)} %get-tuple-element.84.refs_0_.refs_1_.refs_2_, f32[6,288,864]{2,1,0:T(8,128)} %get-tuple-element.84.refs_0_.refs_1_.refs_2_, ...), custom_call_target="tpu_custom_call" | custom-call | bytes 3000000 | tf_op jit(solution)/shard_map/cond/branch_1_fun/pack/pallas_call | solution.py:127
  46.2 2.7 %collective-permute-done.22.refs_4_.refs_5_.refs_6_ = f32[3,48,896]{2,1,0:T(8,128)S(1)} collective-permute-done((f32[3,48,896]{2,1,0:T(8,128)}, f32[3,48,896]{2,1,0:T(8,128)S(1)}, u32[]{:S(2)}, u32[]{:S(2)}) %collective-permute-start.22) | collective-permute-done | bytes 516128 | tf_op jit(solution)/shard_map/cond/branch_1_fun/ppermute | solution.py:342
  48.9 5.2 %collective-permute-done.23.refs_6_.refs_8_.refs_10_ = f32[3,48,896]{2,1,0:T(8,128)S(1)} collective-permute-done((f32[3,48,896]{2,1,0:T(8,128)}, f32[3,48,896]{2,1,0:T(8,128)S(1)}, u32[]{:S(2)}, u32[]{:S(2)}) %collective-permute-start.23) | collective-permute-done | bytes 516128 | tf_op jit(solution)/shard_map/cond/branch_1_fun/ppermute | solution.py:342
  54.9 3.7 %route.18 = (f32[4,48,896]{2,1,0:T(8,128)}, f32[4,48,896]{2,1,0:T(8,128)}, f32[4,48,896]{2,1,0:T(8,128)}) custom-call(s32[281]{0:T(512)S(1)} %get-tuple-element.83.table_ref.refs_0_, f32[3,48,896]{2,1,0:T(8,128)} %get-tuple-element.86.refs_1_, f32[3,48,896]{2,1,0:T(8,128)} %copy-done.18, f32[3,48,896]{2,1,0:T(8,128)} %get-tuple-element.91.refs_3_.refs_4_.refs_5_, ...), custom_call_target="tpu_custom_call" | custom-call | bytes 1600000 | tf_op jit(solution)/shard_map/cond/branch_1_fun/route/pallas_call | solution.py:193
  59.0 2.2 %collective-permute-start.26 = (f32[4,48,896]{2,1,0:T(8,128)}, f32[4,48,896]{2,1,0:T(8,128)S(1)}, u32[]{:S(2)}, u32[]{:S(2)}) collective-permute-start(f32[4,48,896]{2,1,0:T(8,128)} %get-tuple-element.97), channel_id=1, source_target_pairs={{0,64},{16,80},{32,96},{48,112},{64,0},{80,16},{96,32},{112,48},{1... | collective-permute-start | bytes 2064392 | tf_op jit(solution)/shard_map/cond/branch_1_fun/ppermute | solution.py:342
  62.6 2.7 %route.21 = (f32[4,168,128]{2,1,0:T(8,128)}, f32[4,168,128]{2,1,0:T(8,128)}) custom-call(s32[281]{0:T(512)S(1)} %get-tuple-element.83.table_ref.refs_0_, f32[3,336,128]{2,1,0:T(8,128)} %copy-done.15, f32[3,168,128]{2,1,0:T(8,128)} %copy-done.28, f32[3,336,128]{2,1,0:T(8,128)} %copy-done.15, f32[3,168,128]{2,1,0:T(8,128)} %copy-done.27), custom_call_target="tpu_custom_call" | custom-call | bytes 1600000 | tf_op jit(solution)/shard_map/cond/branch_1_fun/route/pallas_call | solution.py:193
  65.6 2.6 %collective-permute-start.37 = (f32[4,168,128]{2,1,0:T(8,128)}, f32[4,168,128]{2,1,0:T(8,128)S(1)}, u32[]{:S(2)}, u32[]{:S(2)}) collective-permute-start(f32[4,168,128]{2,1,0:T(8,128)} %get-tuple-element.116), channel_id=1, source_target_pairs={{0,6},{1,7},{2,4},{3,5},{4,2},{5,3},{6,0},{7,1},{8,14},{9,15},{10,... | collective-permute-start | bytes 1032200 | tf_op jit(solution)/shard_map/cond/branch_1_fun/ppermute | solution.py:342
  68.2 7.1 %collective-permute-done.36.refs_3_ = f32[4,168,128]{2,1,0:T(8,128)S(1)} collective-permute-done((f32[4,168,128]{2,1,0:T(8,128)}, f32[4,168,128]{2,1,0:T(8,128)S(1)}, u32[]{:S(2)}, u32[]{:S(2)}) %collective-permute-start.36) | collective-permute-done | bytes 344096 | tf_op jit(solution)/shard_map/cond/branch_1_fun/ppermute | solution.py:342
  77.4 2.9 %route.22 = (f32[5,168,128]{2,1,0:T(8,128)}, f32[5,168,128]{2,1,0:T(8,128)}) custom-call(s32[281]{0:T(512)S(1)} %get-tuple-element.83.table_ref.refs_0_, f32[3,336,128]{2,1,0:T(8,128)} %copy-done.15, f32[3,168,128]{2,1,0:T(8,128)} %copy-done.28, f32[4,168,128]{2,1,0:T(8,128)} %copy-done.29, f32[3,336,128]{2,1,0:T(8,128)} %copy-done.15, ...), custom_call_target="tpu_custom_call" | custom-call | bytes 2000000 | tf_op jit(solution)/shard_map/cond/branch_1_fun/route/pallas_call | solution.py:193
  80.2 1.9 %collective-permute-start.38 = (f32[5,168,128]{2,1,0:T(8,128)}, f32[5,168,128]{2,1,0:T(8,128)S(1)}, u32[]{:S(2)}, u32[]{:S(2)}) collective-permute-start(f32[5,168,128]{2,1,0:T(8,128)} %get-tuple-element.119), channel_id=1, source_target_pairs={{0,6},{1,7},{2,4},{3,5},{4,2},{5,3},{6,0},{7,1},{8,14},{9,15},{10,... | collective-permute-start | bytes 1290248 | tf_op jit(solution)/shard_map/cond/branch_1_fun/ppermute | solution.py:342
  82.1 2.2 %collective-permute-start.39 = (f32[5,168,128]{2,1,0:T(8,128)}, f32[5,168,128]{2,1,0:T(8,128)S(1)}, u32[]{:S(2)}, u32[]{:S(2)}) collective-permute-start(f32[5,168,128]{2,1,0:T(8,128)} %get-tuple-element.120), channel_id=1, source_target_pairs={{0,8},{1,9},{2,10},{3,11},{4,12},{5,13},{6,14},{7,15},{8,0},{9,1},... | collective-permute-start | bytes 1290248 | tf_op jit(solution)/shard_map/cond/branch_1_fun/ppermute | solution.py:342
  86.3 4.0 %route.19 = (f32[5,48,896]{2,1,0:T(8,128)}, f32[5,48,896]{2,1,0:T(8,128)}, f32[5,48,896]{2,1,0:T(8,128)}) custom-call(s32[281]{0:T(512)S(1)} %get-tuple-element.83.table_ref.refs_0_, f32[3,48,896]{2,1,0:T(8,128)} %get-tuple-element.86.refs_1_, f32[3,48,896]{2,1,0:T(8,128)} %copy-done.18, f32[4,48,896]{2,1,0:T(8,128)} %copy-done.24, ...), custom_call_target="tpu_custom_call" | custom-call | bytes 2000000 | tf_op jit(solution)/shard_map/cond/branch_1_fun/route/pallas_call | solution.py:193
  94.7 3.0 %route.23 = (f32[6,168,128]{2,1,0:T(8,128)}, f32[6,168,128]{2,1,0:T(8,128)}) custom-call(s32[281]{0:T(512)S(1)} %get-tuple-element.83.table_ref.refs_0_, f32[3,336,128]{2,1,0:T(8,128)} %copy-done.15, f32[3,168,128]{2,1,0:T(8,128)} %copy-done.28, f32[4,168,128]{2,1,0:T(8,128)} %copy-done.29, f32[5,168,128]{2,1,0:T(8,128)} %copy-done.38, ...), custom_call_target="tpu_custom_call" | custom-call | bytes 2400000 | tf_op jit(solution)/shard_map/cond/branch_1_fun/route/pallas_call | solution.py:193
  98.3 1.6 collective-permute-done.40.refs_2_
  100.8 6.1 %left.3 = (bf16[6,5,256,256]{3,2,1,0:T(8,128)(2,1)}, bf16[6,5,256,256]{3,2,1,0:T(8,128)(2,1)}, f32[6,8,128]{2,1,0:T(8,128)}) custom-call(s32[1]{0:T(128)} %get-tuple-element.110.core_ref, f32[6,168,128]{2,1,0:T(8,128)} %get-tuple-element.123.refs_0_, f32[6,168,128]{2,1,0:T(8,128)} %get-tuple-element.124.refs_1_, f32[6,168,128]{2,1,0:T(8,128)} %copy-done.37, ...), custom_call_target="tpu_custom_call" | custom-call | bytes 12000000 | tf_op jit(solution)/shard_map/cond/branch_1_fun/left/pallas_call | solution.py:229
  106.9 2.8 %collective-permute-done.27.refs_4_ = f32[5,48,896]{2,1,0:T(8,128)S(1)} collective-permute-done((f32[5,48,896]{2,1,0:T(8,128)}, f32[5,48,896]{2,1,0:T(8,128)S(1)}, u32[]{:S(2)}, u32[]{:S(2)}) %collective-permute-start.27) | collective-permute-done | bytes 860192 | tf_op jit(solution)/shard_map/cond/branch_1_fun/ppermute | solution.py:342
  109.6 1.6 collective-permute-done.28.refs_8_
  113.0 4.3 %route.20 = (f32[6,48,896]{2,1,0:T(8,128)}, f32[6,48,896]{2,1,0:T(8,128)}, f32[6,48,896]{2,1,0:T(8,128)}) custom-call(s32[281]{0:T(512)S(1)} %get-tuple-element.83.table_ref.refs_0_, f32[3,48,896]{2,1,0:T(8,128)} %get-tuple-element.86.refs_1_, f32[3,48,896]{2,1,0:T(8,128)} %copy-done.18, f32[4,48,896]{2,1,0:T(8,128)} %copy-done.24, ...), custom_call_target="tpu_custom_call" | custom-call | bytes 2400000 | tf_op jit(solution)/shard_map/cond/branch_1_fun/route/pallas_call | solution.py:193
  119.4 1.7 %collective-permute-start.32 = (f32[6,48,896]{2,1,0:T(8,128)}, f32[6,48,896]{2,1,0:T(8,128)S(1)}, u32[]{:S(2)}, u32[]{:S(2)}) collective-permute-start(f32[6,48,896]{2,1,0:T(8,128)} %get-tuple-element.109.p2), channel_id=1, source_target_pairs={{0,48},{16,32},{32,16},{48,0},{64,112},{80,96},{96,80},{112,64},{1... | collective-permute-start | bytes 3096584 | tf_op jit(solution)/shard_map/cond/branch_1_fun/ppermute | solution.py:342
  121.2 2.1 %copy-done.3 = bf16[6,5,256,256]{3,2,1,0:T(8,128)(2,1)S(1)} copy-done((bf16[6,5,256,256]{3,2,1,0:T(8,128)(2,1)S(1)}, bf16[6,5,256,256]{3,2,1,0:T(8,128)(2,1)}, u32[]{:S(2)}) %copy-start.3) | copy-done | bytes 3932184 | tf_op jit(solution)/shard_map/cond
  126.9 14.6 %mine.3.part_ref = f32[6,864,640]{2,1,0:T(8,128)} custom-call(bf16[6,864,640]{2,1,0:T(8,128)(2,1)} %get-tuple-element.82.grad_ref, f32[6,48,896]{2,1,0:T(8,128)S(1)} %copy-done.11, f32[6,48,896]{2,1,0:T(8,128)S(1)} %copy-done.9, f32[6,48,896]{2,1,0:T(8,128)S(1)} %copy-done.7, bf16[6,5,256,256]{3,2,1,0:T(8,128)(2,1)S(1)} %copy-done.3, f32[6,8,128]{2,1,0:T(8,128)S(1)} %copy-done.13), custom_call_target="tpu_custom_call" | custom-call | flops 16000000000 | bytes 30000000 | tf_op jit(solution)/shard_map/cond/branch_1_fun/mine/pallas_call | solution.py:310
  141.5 1.6 collective-permute-done.32.p2
  143.1 18.6 %other.3 = bf16[6,864,640]{2,1,0:T(8,128)(2,1)} custom-call(bf16[6,864,640]{2,1,0:T(8,128)(2,1)} %get-tuple-element.82.grad_ref, f32[6,48,896]{2,1,0:T(8,128)S(1)} %collective-permute-done.30.p0, f32[6,48,896]{2,1,0:T(8,128)S(1)} %collective-permute-done.31.p1, f32[6,48,896]{2,1,0:T(8,128)S(1)} %collective-permute-done.32.p2, ...), custom_call_target="tpu_custom_call" | custom-call | flops 20000000000 | bytes 40000000 | tf_op jit(solution)/shard_map/cond/branch_1_fun/other/pallas_call | solution.py:324
  (86 shorter events, 27.4 us)
Async XLA Ops:
  11.6 16.5 %collective-permute-start.33 = (f32[3,336,128]{2,1,0:T(8,128)}, f32[3,336,128]{2,1,0:T(8,128)S(1)}, u32[]{:S(2)}, u32[]{:S(2)}) collective-permute-start(f32[3,336,128]{2,1,0:T(8,128)} %gather.3), channel_id=1, source_target_pairs={{0,0},{1,1},{2,16},{3,17},{4,32},{5,33},{6,48},{7,49},{8,64},{9,65... | collective-permute-start | bytes 1548296 | tf_op jit(solution)/shard_map/cond/branch_1_fun/ppermute | solution.py:352
  17.9 28.2 %collective-permute-start.21 = (f32[3,48,896]{2,1,0:T(8,128)}, f32[3,48,896]{2,1,0:T(8,128)S(1)}, u32[]{:S(2)}, u32[]{:S(2)}) collective-permute-start(f32[3,48,896]{2,1,0:T(8,128)} %get-tuple-element.87), channel_id=1, source_target_pairs={{0,64},{16,80},{32,96},{48,112},{64,0},{80,16},{96,32},{112,48},{1... | collective-permute-start | bytes 1548296 | tf_op jit(solution)/shard_map/cond/branch_1_fun/ppermute | solution.py:342
  21.2 27.7 %collective-permute-start.22 = (f32[3,48,896]{2,1,0:T(8,128)}, f32[3,48,896]{2,1,0:T(8,128)S(1)}, u32[]{:S(2)}, u32[]{:S(2)}) collective-permute-start(f32[3,48,896]{2,1,0:T(8,128)} %get-tuple-element.88), channel_id=1, source_target_pairs={{0,16},{16,0},{32,48},{48,32},{64,80},{80,64},{96,112},{112,96},{1... | collective-permute-start | bytes 1548296 | tf_op jit(solution)/shard_map/cond/branch_1_fun/ppermute | solution.py:342
  24.1 30.0 %collective-permute-start.23 = (f32[3,48,896]{2,1,0:T(8,128)}, f32[3,48,896]{2,1,0:T(8,128)S(1)}, u32[]{:S(2)}, u32[]{:S(2)}) collective-permute-start(f32[3,48,896]{2,1,0:T(8,128)} %get-tuple-element.89), channel_id=1, source_target_pairs={{0,48},{16,32},{32,16},{48,0},{64,112},{80,96},{96,80},{112,64},{1... | collective-permute-start | bytes 1548296 | tf_op jit(solution)/shard_map/cond/branch_1_fun/ppermute | solution.py:342
  28.1 18.1 %copy-start.15 = (f32[3,336,128]{2,1,0:T(8,128)}, f32[3,336,128]{2,1,0:T(8,128)S(1)}, u32[]{:S(2)}) copy-start(f32[3,336,128]{2,1,0:T(8,128)S(1)} %collective-permute-done.33.refs_1_.refs_3_.refs_4_.refs_5_) | copy-start | bytes 1548292 | tf_op jit(solution)/shard_map/cond
  28.9 32.3 %collective-permute-start.35 = (f32[3,168,128]{2,1,0:T(8,128)}, f32[3,168,128]{2,1,0:T(8,128)S(1)}, u32[]{:S(2)}, u32[]{:S(2)}) collective-permute-start(f32[3,168,128]{2,1,0:T(8,128)} %get-tuple-element.144), channel_id=1, source_target_pairs={{0,2},{1,3},{2,0},{3,1},{4,6},{5,7},{6,4},{7,5},{8,10},{9,11},{10,... | collective-permute-start | bytes 774152 | tf_op jit(solution)/shard_map/cond/branch_1_fun/ppermute | solution.py:342
  41.9 19.3 %collective-permute-start.34 = (f32[3,168,128]{2,1,0:T(8,128)S(1)}, f32[3,168,128]{2,1,0:T(8,128)S(1)}, u32[]{:S(2)}, u32[]{:S(2)}) collective-permute-start(f32[3,168,128]{2,1,0:T(8,128)S(1)} %get-tuple-element.145), channel_id=1, source_target_pairs={{0,8},{1,9},{2,10},{3,11},{4,12},{5,13},{6,14},{7,15},{8,0},{9,1},... | collective-permute-start | bytes 774152 | tf_op jit(solution)/shard_map/cond/branch_1_fun/ppermute | solution.py:342
  46.2 7.9 %copy-start.18 = (f32[3,48,896]{2,1,0:T(8,128)}, f32[3,48,896]{2,1,0:T(8,128)S(1)}, u32[]{:S(2)}) copy-start(f32[3,48,896]{2,1,0:T(8,128)S(1)} %collective-permute-done.21.refs_2_) | copy-start | bytes 1548292 | tf_op jit(solution)/shard_map/cond
  48.9 5.2 %copy-start.19 = (f32[3,48,896]{2,1,0:T(8,128)}, f32[3,48,896]{2,1,0:T(8,128)S(1)}, u32[]{:S(2)}) copy-start(f32[3,48,896]{2,1,0:T(8,128)S(1)} %collective-permute-done.22.refs_4_.refs_5_.refs_6_) | copy-start | bytes 1548292 | tf_op jit(solution)/shard_map/cond
  58.7 25.6 %collective-permute-start.24 = (f32[4,48,896]{2,1,0:T(8,128)}, f32[4,48,896]{2,1,0:T(8,128)S(1)}, u32[]{:S(2)}, u32[]{:S(2)}) collective-permute-start(f32[4,48,896]{2,1,0:T(8,128)} %get-tuple-element.95), channel_id=1, source_target_pairs={{0,16},{16,0},{32,48},{48,32},{64,80},{80,64},{96,112},{112,96},{1... | collective-permute-start | bytes 2064392 | tf_op jit(solution)/shard_map/cond/branch_1_fun/ppermute | solution.py:342
  58.8 25.5 %collective-permute-start.25 = (f32[4,48,896]{2,1,0:T(8,128)}, f32[4,48,896]{2,1,0:T(8,128)S(1)}, u32[]{:S(2)}, u32[]{:S(2)}) collective-permute-start(f32[4,48,896]{2,1,0:T(8,128)} %get-tuple-element.96), channel_id=1, source_target_pairs={{0,48},{16,32},{32,16},{48,0},{64,112},{80,96},{96,80},{112,64},{1... | collective-permute-start | bytes 2064392 | tf_op jit(solution)/shard_map/cond/branch_1_fun/ppermute | solution.py:342
  59.0 25.3 %collective-permute-start.26 = (f32[4,48,896]{2,1,0:T(8,128)}, f32[4,48,896]{2,1,0:T(8,128)S(1)}, u32[]{:S(2)}, u32[]{:S(2)}) collective-permute-start(f32[4,48,896]{2,1,0:T(8,128)} %get-tuple-element.97), channel_id=1, source_target_pairs={{0,64},{16,80},{32,96},{48,112},{64,0},{80,16},{96,32},{112,48},{1... | collective-permute-start | bytes 2064392 | tf_op jit(solution)/shard_map/cond/branch_1_fun/ppermute | solution.py:342
  65.4 10.0 %collective-permute-start.36 = (f32[4,168,128]{2,1,0:T(8,128)}, f32[4,168,128]{2,1,0:T(8,128)S(1)}, u32[]{:S(2)}, u32[]{:S(2)}) collective-permute-start(f32[4,168,128]{2,1,0:T(8,128)} %get-tuple-element.115), channel_id=1, source_target_pairs={{0,2},{1,3},{2,0},{3,1},{4,6},{5,7},{6,4},{7,5},{8,10},{9,11},{10,... | collective-permute-start | bytes 1032200 | tf_op jit(solution)/shard_map/cond/branch_1_fun/ppermute | solution.py:342
  65.6 11.1 %collective-permute-start.37 = (f32[4,168,128]{2,1,0:T(8,128)}, f32[4,168,128]{2,1,0:T(8,128)S(1)}, u32[]{:S(2)}, u32[]{:S(2)}) collective-permute-start(f32[4,168,128]{2,1,0:T(8,128)} %get-tuple-element.116), channel_id=1, source_target_pairs={{0,6},{1,7},{2,4},{3,5},{4,2},{5,3},{6,0},{7,1},{8,14},{9,15},{10,... | collective-permute-start | bytes 1032200 | tf_op jit(solution)/shard_map/cond/branch_1_fun/ppermute | solution.py:342
  75.3 1.3 copy-start.29
  80.2 12.6 %collective-permute-start.38 = (f32[5,168,128]{2,1,0:T(8,128)}, f32[5,168,128]{2,1,0:T(8,128)S(1)}, u32[]{:S(2)}, u32[]{:S(2)}) collective-permute-start(f32[5,168,128]{2,1,0:T(8,128)} %get-tuple-element.119), channel_id=1, source_target_pairs={{0,6},{1,7},{2,4},{3,5},{4,2},{5,3},{6,0},{7,1},{8,14},{9,15},{10,... | collective-permute-start | bytes 1290248 | tf_op jit(solution)/shard_map/cond/branch_1_fun/ppermute | solution.py:342
  82.1 11.8 %collective-permute-start.39 = (f32[5,168,128]{2,1,0:T(8,128)}, f32[5,168,128]{2,1,0:T(8,128)S(1)}, u32[]{:S(2)}, u32[]{:S(2)}) collective-permute-start(f32[5,168,128]{2,1,0:T(8,128)} %get-tuple-element.120), channel_id=1, source_target_pairs={{0,8},{1,9},{2,10},{3,11},{4,12},{5,13},{6,14},{7,15},{8,0},{9,1},... | collective-permute-start | bytes 1290248 | tf_op jit(solution)/shard_map/cond/branch_1_fun/ppermute | solution.py:342
  90.3 19.3 %collective-permute-start.27 = (f32[5,48,896]{2,1,0:T(8,128)}, f32[5,48,896]{2,1,0:T(8,128)S(1)}, u32[]{:S(2)}, u32[]{:S(2)}) collective-permute-start(f32[5,48,896]{2,1,0:T(8,128)} %get-tuple-element.101), channel_id=1, source_target_pairs={{0,48},{16,32},{32,16},{48,0},{64,112},{80,96},{96,80},{112,64},{1... | collective-permute-start | bytes 2580488 | tf_op jit(solution)/shard_map/cond/branch_1_fun/ppermute | solution.py:342
  91.3 19.9 %collective-permute-start.28 = (f32[5,48,896]{2,1,0:T(8,128)}, f32[5,48,896]{2,1,0:T(8,128)S(1)}, u32[]{:S(2)}, u32[]{:S(2)}) collective-permute-start(f32[5,48,896]{2,1,0:T(8,128)} %get-tuple-element.102), channel_id=1, source_target_pairs={{0,64},{16,80},{32,96},{48,112},{64,0},{80,16},{96,32},{112,48},{1... | collective-permute-start | bytes 2580488 | tf_op jit(solution)/shard_map/cond/branch_1_fun/ppermute | solution.py:342
  92.4 19.0 %collective-permute-start.29 = (f32[5,48,896]{2,1,0:T(8,128)}, f32[5,48,896]{2,1,0:T(8,128)S(1)}, u32[]{:S(2)}, u32[]{:S(2)}) collective-permute-start(f32[5,48,896]{2,1,0:T(8,128)} %get-tuple-element.103), channel_id=1, source_target_pairs={{0,16},{16,0},{32,48},{48,32},{64,80},{80,64},{96,112},{112,96},{1... | collective-permute-start | bytes 2580488 | tf_op jit(solution)/shard_map/cond/branch_1_fun/ppermute | solution.py:342
  97.7 2.2 %collective-permute-start.40 = (f32[6,168,128]{2,1,0:T(8,128)}, f32[6,168,128]{2,1,0:T(8,128)S(1)}, u32[]{:S(2)}, u32[]{:S(2)}) collective-permute-start(f32[6,168,128]{2,1,0:T(8,128)} %get-tuple-element.123.refs_0_), channel_id=1, source_target_pairs={{0,1},{1,0},{2,3},{3,2},{4,5},{5,4},{6,7},{7,6},{8,9},{9,8},{10,11... | collective-permute-start | bytes 1548296 | tf_op jit(solution)/shard_map/cond/branch_1_fun/ppermute | solution.py:370
  97.8 3.0 %collective-permute-start.41 = (f32[6,168,128]{2,1,0:T(8,128)}, f32[6,168,128]{2,1,0:T(8,128)}, u32[]{:S(2)}, u32[]{:S(2)}) collective-permute-start(f32[6,168,128]{2,1,0:T(8,128)} %get-tuple-element.124.refs_1_), channel_id=1, source_target_pairs={{0,1},{1,0},{2,3},{3,2},{4,5},{5,4},{6,7},{7,6},{8,9},{9,8},{10,11... | collective-permute-start | bytes 1548296 | tf_op jit(solution)/shard_map/cond/branch_1_fun/ppermute | solution.py:370
  106.9 14.3 %copy-start.13 = (f32[6,8,128]{2,1,0:T(8,128)S(1)}, f32[6,8,128]{2,1,0:T(8,128)}, u32[]{:S(2)}) copy-start(f32[6,8,128]{2,1,0:T(8,128)} %get-tuple-element.126.a_ref) | copy-start | bytes 73732 | tf_op jit(solution)/shard_map/cond
  109.6 1.8 %copy-start.34 = (f32[5,48,896]{2,1,0:T(8,128)}, f32[5,48,896]{2,1,0:T(8,128)S(1)}, u32[]{:S(2)}) copy-start(f32[5,48,896]{2,1,0:T(8,128)S(1)} %collective-permute-done.27.refs_4_) | copy-start | bytes 2580484 | tf_op jit(solution)/shard_map/cond
  117.4 24.2 %collective-permute-start.30 = (f32[6,48,896]{2,1,0:T(8,128)}, f32[6,48,896]{2,1,0:T(8,128)S(1)}, u32[]{:S(2)}, u32[]{:S(2)}) collective-permute-start(f32[6,48,896]{2,1,0:T(8,128)} %get-tuple-element.107.p0), channel_id=1, source_target_pairs={{0,64},{16,80},{32,96},{48,112},{64,0},{80,16},{96,32},{112,48},{1... | collective-permute-start | bytes 3096584 | tf_op jit(solution)/shard_map/cond/branch_1_fun/ppermute | solution.py:342
  118.1 23.5 %collective-permute-start.31 = (f32[6,48,896]{2,1,0:T(8,128)}, f32[6,48,896]{2,1,0:T(8,128)S(1)}, u32[]{:S(2)}, u32[]{:S(2)}) collective-permute-start(f32[6,48,896]{2,1,0:T(8,128)} %get-tuple-element.108.p1), channel_id=1, source_target_pairs={{0,16},{16,0},{32,48},{48,32},{64,80},{80,64},{96,112},{112,96},{1... | collective-permute-start | bytes 3096584 | tf_op jit(solution)/shard_map/cond/branch_1_fun/ppermute | solution.py:342
  119.4 23.7 %collective-permute-start.32 = (f32[6,48,896]{2,1,0:T(8,128)}, f32[6,48,896]{2,1,0:T(8,128)S(1)}, u32[]{:S(2)}, u32[]{:S(2)}) collective-permute-start(f32[6,48,896]{2,1,0:T(8,128)} %get-tuple-element.109.p2), channel_id=1, source_target_pairs={{0,48},{16,32},{32,16},{48,0},{64,112},{80,96},{96,80},{112,64},{1... | collective-permute-start | bytes 3096584 | tf_op jit(solution)/shard_map/cond/branch_1_fun/ppermute | solution.py:342
  121.2 2.1 %copy-start.3 = (bf16[6,5,256,256]{3,2,1,0:T(8,128)(2,1)S(1)}, bf16[6,5,256,256]{3,2,1,0:T(8,128)(2,1)}, u32[]{:S(2)}) copy-start(bf16[6,5,256,256]{3,2,1,0:T(8,128)(2,1)} %get-tuple-element.125.first_ref) | copy-start | bytes 11796484 | tf_op jit(solution)/shard_map/cond
  123.3 1.2 copy-start.7
  124.5 1.2 copy-start.9
  126.9 16.2 %copy-start.4 = (bf16[6,5,256,256]{3,2,1,0:T(8,128)(2,1)S(1)}, bf16[6,5,256,256]{3,2,1,0:T(8,128)(2,1)}, u32[]{:S(2)}) copy-start(bf16[6,5,256,256]{3,2,1,0:T(8,128)(2,1)} %get-tuple-element.125.first_ref) | copy-start | bytes 11796484 | tf_op jit(solution)/shard_map/cond
  126.9 16.2 %copy-start.5 = (bf16[6,5,256,256]{3,2,1,0:T(8,128)(2,1)S(1)}, bf16[6,5,256,256]{3,2,1,0:T(8,128)(2,1)}, u32[]{:S(2)}) copy-start(bf16[6,5,256,256]{3,2,1,0:T(8,128)(2,1)} %get-tuple-element.127.second_ref) | copy-start | bytes 11796484 | tf_op jit(solution)/shard_map/cond
  (13 other events, 11.5 us)
